TPU v7x, 128 devices: a whole 4x4x4 slice. The times are simulated.
128 devices in a mesh: cent: 32 (over x, y, core), qry: 4 (over z).
Axes of the slice: x: 4, y: 4, z: 4, core: 2. Of those that a mesh axis runs over, the one named last changes fastest.
Arguments:
- queries: bfloat16 [4, 128, 32, 128], P('qry', 'cent'), may hold values from -0.75 to 0.75
- centroids: bfloat16 [1048576, 128], P('cent'), may hold values from -0.5 to 0.5
- shard_table: int32 [32, 16384], P('cent'), may hold values from 0 to 32767
- token_refs: int32 [4096, 128], P('cent'), may hold values from 0 to 16383
- packed_residual_buckets: int32 [4096, 16, 128], P('cent'), may hold values from 0 to 65280
- passage_lengths: int32 [4096], P('cent'), may hold values from 1 to 128
- bucket_values: float32 [4, 128], replicated, may hold values from -0.75 to 0.75
- candidates: int32 [4, 32, 128, 48], P('qry', 'cent'), may hold values from 0 to 127
- live_counts: int32 [4, 32, 128], P('qry', 'cent'), may hold values from 12 to 36, as said below
Outputs:
- shard_tops: float32 [4, 128, 32, 12], P('qry', 'cent')
- best_scores: float32 [4, 128, 100], P('qry', 'cent')
Inputs may be any that keep to these rules, and one draw needn't show every extreme that they name: The bucket of dimension k * 16 + j of token t of passage n is floor(packed_residual_buckets[n, j, t] / 4**k) mod 4, for k = 0..7. Slots 0 to live_counts - 1 of a query's list on a shard are live, the rest padding. On every shard, query i and query 128 - 1 - i of a group hold 48 live slots together, so each device holds 3072 live slots.
All inputs are finite; a program needn't handle non-finite values.
Results may differ from a plain program's by a relative error of at most 0.0003.
Values may be sent and summed in bfloat16 or wider, within the bound.
A program may use at most 128 MiB of HBM per device.

v0:
```python
import math

import jax
import jax.numpy as jnp
import numpy as np
from jax import lax
from jax.sharding import PartitionSpec as P

TOPK = 100


NEG = -1e30
EPS = 1e-06


def decode_shard(packed_word_bits, token_refs, bucket_values, tablevec):
    powers = jnp.asarray(np.array([4**k for k in range(8)], dtype=np.int32))
    digits = packed_word_bits[:, None, :, :] // powers[None, :, None, None] % 4
    digits = digits.reshape(packed_word_bits.shape[0], -1, packed_word_bits.shape[2])
    residual = jnp.zeros(digits.shape, jnp.float32)
    for residual_bucket_number in range(4):
        residual = residual + jnp.where(
            digits == residual_bucket_number,
            bucket_values[residual_bucket_number][None, :, None],
            0.0,
        )
    cent_tok = jnp.swapaxes(jnp.take(tablevec, token_refs, axis=0), 1, 2).astype(jnp.float32)
    summed = cent_tok + residual
    inverse_norm = lax.rsqrt(jnp.sum(summed * summed, axis=1, keepdims=True) + EPS)
    return (summed * inverse_norm).astype(jnp.bfloat16)


def local(
    queries,
    centroids,
    shard_table,
    token_refs,
    packed_residual_buckets,
    passage_lengths,
    bucket_values,
    candidates,
    live_counts,
):
    shards = lax.axis_size("cent")
    qry_dev = queries.shape[1]
    group_rows = lax.all_gather(queries, "cent", axis=1, tiled=True)[0]
    wanted = shard_table[0].reshape(shards, -1)
    fetched = jnp.take(
        centroids, lax.all_to_all(wanted, "cent", split_axis=0, concat_axis=0, tiled=True), axis=0
    )
    vectors = lax.all_to_all(fetched, "cent", split_axis=0, concat_axis=0, tiled=True)
    tablevec = vectors.reshape(-1, vectors.shape[2])
    embeds = decode_shard(packed_residual_buckets, token_refs, bucket_values, tablevec)
    passage_count = embeds.shape[0]
    valid_tok = (
        jnp.arange(packed_residual_buckets.shape[2], dtype=jnp.int32)[None, :]
        < passage_lengths[:, None]
    )
    slot_cand = candidates[0, 0]
    slot_count = live_counts[0, 0]
    qcount, slots = slot_cand.shape
    live_grid = jnp.arange(slots, dtype=jnp.int32)[None, :] < slot_count[:, None]
    query_block = math.gcd(qcount, 8)

    def query_block_scores(first_row):
        query_tile_rows = lax.dynamic_slice_in_dim(group_rows, first_row, query_block, 0)
        similarity_matrix = jnp.einsum(
            "qtd,pdj->qtpj", query_tile_rows, embeds, preferred_element_type=jnp.float32
        )
        similarity_matrix = jnp.where(valid_tok[None, None, :, :], similarity_matrix, NEG)
        return jnp.sum(jnp.max(similarity_matrix, axis=3), axis=1)

    block_starts = jnp.arange(qcount // query_block, dtype=jnp.int32) * query_block
    passage_scores = lax.map(query_block_scores, block_starts).reshape(qcount, passage_count)
    chosen = slot_cand[:, :, None] == jnp.arange(passage_count, dtype=jnp.int32)[None, None, :]
    picked = jnp.sum(jnp.where(chosen, passage_scores[:, None, :], 0.0), axis=2)
    scores = jnp.where(live_grid, picked, NEG)
    keep_count = slots // 4
    local_tops = lax.top_k(scores, keep_count)[0]
    all_tops = lax.all_gather(local_tops[None], "cent", axis=0, tiled=True)
    arrived = lax.dynamic_slice_in_dim(all_tops, lax.axis_index("cent") * qry_dev, qry_dev, 1)
    shard_tops = jnp.swapaxes(arrived, 0, 1)
    best_scores = lax.top_k(shard_tops.reshape(qry_dev, -1), TOPK)[0]
    return (shard_tops[None], best_scores[None])


def solution(mesh):
    return jax.shard_map(
        local,
        mesh=mesh,
        in_specs=(
            P("qry", "cent", None, None),
            P("cent", None),
            P("cent", None),
            P("cent", None),
            P("cent", None, None),
            P("cent"),
            P(),
            P("qry", "cent", None, None),
            P("qry", "cent", None),
        ),
        out_specs=(P("qry", "cent", None, None), P("qry", "cent", None)),
        check_vma=False,
    )
```

profile of v0, /device:TPU:1, one launch (start us, length us, event | category | flops | bytes accessed | tf_op | source)
XLA Modules:
  0.0 521.3 jit_solution(10099032033358095141)
XLA Ops:
  7.2 16.0 %all_to_all.20 = s32[32,1,512]{2,1,0:T(1,128)S(1)} all-to-all(s32[32,1,512]{2,1,0:T(1,128)} %bitcast.88), channel_id=1, replica_groups=mesh['cent'=32,'qry'=4] {'cent'}, dimensions={0} | all-to-all | bytes 131072 | tf_op jit(solution)/shard_map/all_to_all | solution.py:49
  23.2 59.4 %gather_fusion = bf16[16384,128]{1,0:T(8,128)(2,1)} fusion(bf16[32768,128]{1,0:T(8,128)(2,1)} %param.13, s32[16384]{0:T(1024)S(1)} %broadcast_clamp_fusion), kind=kCustom, calls=%fused_computation | custom fusion | bytes 8454144 | tf_op jit(solution)/shard_map/jit(_take)/gather | solution.py:48
  82.7 7.8 %broadcast_select_fusion = bf16[32,512,128]{2,1,0:T(8,128)(2,1)} fusion(bf16[32,512,128]{2,1,0:T(8,128)(2,1)} %bitcast.82, pred[32,512]{1,0:T(8,128)(4,1)S(1)} %compare_and_fusion), kind=kLoop, calls=%fused_computation.22 | loop fusion | flops 2097152 | bytes 8404992 | tf_op jit(solution)/shard_map/jit(_take)/select_n | solution.py:48
  90.5 4.8 all-to-all-start.1
  95.3 0.7 all-gather.3.cloned.1.call-update
  96.7 51.4 %all-to-all-done.1 = bf16[32,512,128]{2,1,0:T(8,128)(2,1)} async-done(((bf16[32,512,128]{2,1,0:T(8,128)(2,1)}), bf16[32,512,128]{2,1,0:T(8,128)(2,1)}, u32[]{:S(2)}, u32[]{:S(2)}) %all-to-all-start.1) | async-done | bytes 4194336 | tf_op jit(solution)/shard_map/all_to_all | solution.py:51
  148.1 57.7 %gather_fusion.1 = bf16[16384,128]{1,0:T(8,128)(2,1)} fusion(bf16[16384,128]{1,0:T(8,128)(2,1)} %bitcast.8, s32[16384]{0:T(1024)S(1)} %bitcast_clamp_fusion), kind=kCustom, calls=%fused_computation.1 | custom fusion | bytes 8454144 | tf_op jit(solution)/shard_map/jit(_take)/gather | solution.py:27
  205.7 6.4 %copy.25 = bf16[128,128,128]{1,2,0:T(8,128)(2,1)} copy(bf16[128,128,128]{2,1,0:T(8,128)(2,1)} %bitcast.83) | data formatting | bytes 8388608 | tf_op jit(solution)/shard_map/jit(_take)/gather | solution.py:27
  212.1 109.0 %multiply_reduce_fusion = (f32[128,128]{1,0:T(8,128)S(1)}, f32[128,128,128]{2,1,0:T(8,128)S(1)}) fusion(f32[128]{0:T(128)S(1)} %get-tuple-element.80, f32[128]{0:T(128)S(1)} %get-tuple-element.81, f32[128]{0:T(128)S(1)} %get-tuple-element.79, f32[128]{0:T(128)S(1)} %get-tuple-element.78, s32[128]{0:T(128)S(1)} %rem.51, s32[128,16,128]{2,1,0:T(8,128)S(1)} %copy-done, ...), kind=kLoop, calls=%fused_computation.20 | loop fusion | flops 69189632 | bytes 13978112 | tf_op jit(solution)/shard_map/reduce_sum | solution.py:29
  321.2 3.2 multiply_convert_fusion
  324.4 155.4 %while.11 = (s32[]{:T(128)}, f32[16,8,128]{2,1,0:T(8,128)S(1)}, s32[16]{0:T(128)S(1)}, bf16[128,32,128]{2,1,0:T(8,128)(2,1)}, bf16[128,128,128]{2,1,0:T(8,128)(2...) while((s32[]{:T(128)}, f32[16,8,128]{2,1,0:T(8,128)S(1)}, ...), condition=%wide.region_4.5_spmd.clone, body=%wide.region_1.4_spmd.clone.sunk | while | flops 1082145792 | bytes 4567711 | solution.py:74
  327.0 6.8 %select_reduce_fusion.3 = f32[8,32,128]{1,2,0:T(8,128)S(1)} fusion(pred[128,128]{1,0:T(8,128)(4,1)S(1)} %iota_compare_fusion.4, bf16[128,128,128]{2,1,0:T(8,128)(2,1)} %get-tuple-element.143, bf16[128,32,128]{2,1,0:T(8,128)(2,1)} %get-tuple-element.142, s32[]{:T(128)S(6)} %select_n.128), kind=kOutput, calls=%fused_computation.3.clone.1 | convolution fusion | flops 1082097664 | bytes 4407300 | tf_op jit(solution)/shard_map/while/body/eval_jaxpr/qtd,pdj->qtpj/dot_general | solution.py:67
  336.7 6.8 %select_reduce_fusion.3 = f32[8,32,128]{1,2,0:T(8,128)S(1)} fusion(pred[128,128]{1,0:T(8,128)(4,1)S(1)} %iota_compare_fusion.4, bf16[128,128,128]{2,1,0:T(8,128)(2,1)} %get-tuple-element.143, bf16[128,32,128]{2,1,0:T(8,128)(2,1)} %get-tuple-element.142, s32[]{:T(128)S(6)} %select_n.128), kind=kOutput, calls=%fused_computation.3.clone.1 | convolution fusion | flops 1082097664 | bytes 4407300 | tf_op jit(solution)/shard_map/while/body/eval_jaxpr/qtd,pdj->qtpj/dot_general | solution.py:67
  346.5 6.8 %select_reduce_fusion.3 = f32[8,32,128]{1,2,0:T(8,128)S(1)} fusion(pred[128,128]{1,0:T(8,128)(4,1)S(1)} %iota_compare_fusion.4, bf16[128,128,128]{2,1,0:T(8,128)(2,1)} %get-tuple-element.143, bf16[128,32,128]{2,1,0:T(8,128)(2,1)} %get-tuple-element.142, s32[]{:T(128)S(6)} %select_n.128), kind=kOutput, calls=%fused_computation.3.clone.1 | convolution fusion | flops 1082097664 | bytes 4407300 | tf_op jit(solution)/shard_map/while/body/eval_jaxpr/qtd,pdj->qtpj/dot_general | solution.py:67
  356.2 6.8 %select_reduce_fusion.3 = f32[8,32,128]{1,2,0:T(8,128)S(1)} fusion(pred[128,128]{1,0:T(8,128)(4,1)S(1)} %iota_compare_fusion.4, bf16[128,128,128]{2,1,0:T(8,128)(2,1)} %get-tuple-element.143, bf16[128,32,128]{2,1,0:T(8,128)(2,1)} %get-tuple-element.142, s32[]{:T(128)S(6)} %select_n.128), kind=kOutput, calls=%fused_computation.3.clone.1 | convolution fusion | flops 1082097664 | bytes 4407300 | tf_op jit(solution)/shard_map/while/body/eval_jaxpr/qtd,pdj->qtpj/dot_general | solution.py:67
  365.9 6.8 %select_reduce_fusion.3 = f32[8,32,128]{1,2,0:T(8,128)S(1)} fusion(pred[128,128]{1,0:T(8,128)(4,1)S(1)} %iota_compare_fusion.4, bf16[128,128,128]{2,1,0:T(8,128)(2,1)} %get-tuple-element.143, bf16[128,32,128]{2,1,0:T(8,128)(2,1)} %get-tuple-element.142, s32[]{:T(128)S(6)} %select_n.128), kind=kOutput, calls=%fused_computation.3.clone.1 | convolution fusion | flops 1082097664 | bytes 4407300 | tf_op jit(solution)/shard_map/while/body/eval_jaxpr/qtd,pdj->qtpj/dot_general | solution.py:67
  375.6 6.8 %select_reduce_fusion.3 = f32[8,32,128]{1,2,0:T(8,128)S(1)} fusion(pred[128,128]{1,0:T(8,128)(4,1)S(1)} %iota_compare_fusion.4, bf16[128,128,128]{2,1,0:T(8,128)(2,1)} %get-tuple-element.143, bf16[128,32,128]{2,1,0:T(8,128)(2,1)} %get-tuple-element.142, s32[]{:T(128)S(6)} %select_n.128), kind=kOutput, calls=%fused_computation.3.clone.1 | convolution fusion | flops 1082097664 | bytes 4407300 | tf_op jit(solution)/shard_map/while/body/eval_jaxpr/qtd,pdj->qtpj/dot_general | solution.py:67
  385.3 6.8 %select_reduce_fusion.3 = f32[8,32,128]{1,2,0:T(8,128)S(1)} fusion(pred[128,128]{1,0:T(8,128)(4,1)S(1)} %iota_compare_fusion.4, bf16[128,128,128]{2,1,0:T(8,128)(2,1)} %get-tuple-element.143, bf16[128,32,128]{2,1,0:T(8,128)(2,1)} %get-tuple-element.142, s32[]{:T(128)S(6)} %select_n.128), kind=kOutput, calls=%fused_computation.3.clone.1 | convolution fusion | flops 1082097664 | bytes 4407300 | tf_op jit(solution)/shard_map/while/body/eval_jaxpr/qtd,pdj->qtpj/dot_general | solution.py:67
  395.0 6.8 %select_reduce_fusion.3 = f32[8,32,128]{1,2,0:T(8,128)S(1)} fusion(pred[128,128]{1,0:T(8,128)(4,1)S(1)} %iota_compare_fusion.4, bf16[128,128,128]{2,1,0:T(8,128)(2,1)} %get-tuple-element.143, bf16[128,32,128]{2,1,0:T(8,128)(2,1)} %get-tuple-element.142, s32[]{:T(128)S(6)} %select_n.128), kind=kOutput, calls=%fused_computation.3.clone.1 | convolution fusion | flops 1082097664 | bytes 4407300 | tf_op jit(solution)/shard_map/while/body/eval_jaxpr/qtd,pdj->qtpj/dot_general | solution.py:67
  404.7 6.8 %select_reduce_fusion.3 = f32[8,32,128]{1,2,0:T(8,128)S(1)} fusion(pred[128,128]{1,0:T(8,128)(4,1)S(1)} %iota_compare_fusion.4, bf16[128,128,128]{2,1,0:T(8,128)(2,1)} %get-tuple-element.143, bf16[128,32,128]{2,1,0:T(8,128)(2,1)} %get-tuple-element.142, s32[]{:T(128)S(6)} %select_n.128), kind=kOutput, calls=%fused_computation.3.clone.1 | convolution fusion | flops 1082097664 | bytes 4407300 | tf_op jit(solution)/shard_map/while/body/eval_jaxpr/qtd,pdj->qtpj/dot_general | solution.py:67
  414.4 6.8 %select_reduce_fusion.3 = f32[8,32,128]{1,2,0:T(8,128)S(1)} fusion(pred[128,128]{1,0:T(8,128)(4,1)S(1)} %iota_compare_fusion.4, bf16[128,128,128]{2,1,0:T(8,128)(2,1)} %get-tuple-element.143, bf16[128,32,128]{2,1,0:T(8,128)(2,1)} %get-tuple-element.142, s32[]{:T(128)S(6)} %select_n.128), kind=kOutput, calls=%fused_computation.3.clone.1 | convolution fusion | flops 1082097664 | bytes 4407300 | tf_op jit(solution)/shard_map/while/body/eval_jaxpr/qtd,pdj->qtpj/dot_general | solution.py:67
  424.2 6.8 %select_reduce_fusion.3 = f32[8,32,128]{1,2,0:T(8,128)S(1)} fusion(pred[128,128]{1,0:T(8,128)(4,1)S(1)} %iota_compare_fusion.4, bf16[128,128,128]{2,1,0:T(8,128)(2,1)} %get-tuple-element.143, bf16[128,32,128]{2,1,0:T(8,128)(2,1)} %get-tuple-element.142, s32[]{:T(128)S(6)} %select_n.128), kind=kOutput, calls=%fused_computation.3.clone.1 | convolution fusion | flops 1082097664 | bytes 4407300 | tf_op jit(solution)/shard_map/while/body/eval_jaxpr/qtd,pdj->qtpj/dot_general | solution.py:67
  433.9 6.8 %select_reduce_fusion.3 = f32[8,32,128]{1,2,0:T(8,128)S(1)} fusion(pred[128,128]{1,0:T(8,128)(4,1)S(1)} %iota_compare_fusion.4, bf16[128,128,128]{2,1,0:T(8,128)(2,1)} %get-tuple-element.143, bf16[128,32,128]{2,1,0:T(8,128)(2,1)} %get-tuple-element.142, s32[]{:T(128)S(6)} %select_n.128), kind=kOutput, calls=%fused_computation.3.clone.1 | convolution fusion | flops 1082097664 | bytes 4407300 | tf_op jit(solution)/shard_map/while/body/eval_jaxpr/qtd,pdj->qtpj/dot_general | solution.py:67
  443.6 6.8 %select_reduce_fusion.3 = f32[8,32,128]{1,2,0:T(8,128)S(1)} fusion(pred[128,128]{1,0:T(8,128)(4,1)S(1)} %iota_compare_fusion.4, bf16[128,128,128]{2,1,0:T(8,128)(2,1)} %get-tuple-element.143, bf16[128,32,128]{2,1,0:T(8,128)(2,1)} %get-tuple-element.142, s32[]{:T(128)S(6)} %select_n.128), kind=kOutput, calls=%fused_computation.3.clone.1 | convolution fusion | flops 1082097664 | bytes 4407300 | tf_op jit(solution)/shard_map/while/body/eval_jaxpr/qtd,pdj->qtpj/dot_general | solution.py:67
  453.3 6.8 %select_reduce_fusion.3 = f32[8,32,128]{1,2,0:T(8,128)S(1)} fusion(pred[128,128]{1,0:T(8,128)(4,1)S(1)} %iota_compare_fusion.4, bf16[128,128,128]{2,1,0:T(8,128)(2,1)} %get-tuple-element.143, bf16[128,32,128]{2,1,0:T(8,128)(2,1)} %get-tuple-element.142, s32[]{:T(128)S(6)} %select_n.128), kind=kOutput, calls=%fused_computation.3.clone.1 | convolution fusion | flops 1082097664 | bytes 4407300 | tf_op jit(solution)/shard_map/while/body/eval_jaxpr/qtd,pdj->qtpj/dot_general | solution.py:67
  463.0 6.8 %select_reduce_fusion.3 = f32[8,32,128]{1,2,0:T(8,128)S(1)} fusion(pred[128,128]{1,0:T(8,128)(4,1)S(1)} %iota_compare_fusion.4, bf16[128,128,128]{2,1,0:T(8,128)(2,1)} %get-tuple-element.143, bf16[128,32,128]{2,1,0:T(8,128)(2,1)} %get-tuple-element.142, s32[]{:T(128)S(6)} %select_n.128), kind=kOutput, calls=%fused_computation.3.clone.1 | convolution fusion | flops 1082097664 | bytes 4407300 | tf_op jit(solution)/shard_map/while/body/eval_jaxpr/qtd,pdj->qtpj/dot_general | solution.py:67
  472.7 6.8 %select_reduce_fusion.3 = f32[8,32,128]{1,2,0:T(8,128)S(1)} fusion(pred[128,128]{1,0:T(8,128)(4,1)S(1)} %iota_compare_fusion.4, bf16[128,128,128]{2,1,0:T(8,128)(2,1)} %get-tuple-element.143, bf16[128,32,128]{2,1,0:T(8,128)(2,1)} %get-tuple-element.142, s32[]{:T(128)S(6)} %select_n.128), kind=kOutput, calls=%fused_computation.3.clone.1 | convolution fusion | flops 1082097664 | bytes 4407300 | tf_op jit(solution)/shard_map/while/body/eval_jaxpr/qtd,pdj->qtpj/dot_general | solution.py:67
  479.8 2.1 select_reduce_fusion.1
  482.1 1.1 top_k.14
  483.2 25.0 %all-gather = f32[4096,12]{0,1:T(8,128)S(1)} all-gather(f32[128,12]{0,1:T(8,128)S(1)} %top_k.15), channel_id=2, replica_groups=mesh['cent'=32,'qry'=4] {'cent'}, dimensions={0}, use_global_device_ids=true | all-gather | bytes 202752 | tf_op jit(solution)/shard_map/all_gather | solution.py:80
  508.8 3.9 top_k.20
  513.3 0.7 copy.28
  (104 shorter events, 16.3 us)
Async XLA Ops:
  82.6 13.4 %copy-start.6 = (s32[8]{0:T(128)S(1)}, s32[8]{0:T(128)}, u32[]{:S(2)}) copy-start(s32[8]{0:T(128)} %constant.106.clone) | copy-start | bytes 100
  82.7 13.6 %copy-start.2 = (s32[1,1,128,48]{2,3,1,0:T(8,128)S(1)}, s32[1,1,128,48]{2,3,1,0:T(8,128)}, u32[]{:S(2)}) copy-start(s32[1,1,128,48]{2,3,1,0:T(8,128)} %param.19) | copy-start | bytes 73732
  82.7 13.7 %copy-start.4 = (f32[4,128]{1,0:T(4,128)S(1)}, f32[4,128]{1,0:T(4,128)}, u32[]{:S(2)}) copy-start(f32[4,128]{1,0:T(4,128)} %param.18) | copy-start | bytes 6148
  82.7 13.7 %copy-start.1 = (s32[128,128]{1,0:T(8,128)S(1)}, s32[128,128]{1,0:T(8,128)}, u32[]{:S(2)}) copy-start(s32[128,128]{1,0:T(8,128)} %param.15) | copy-start | bytes 196612
  82.7 13.7 %copy-start = (s32[128,16,128]{2,1,0:T(8,128)S(1)}, s32[128,16,128]{2,1,0:T(8,128)}, u32[]{:S(2)}) copy-start(s32[128,16,128]{2,1,0:T(8,128)} %param.16) | copy-start | bytes 3145732
  90.5 57.6 %all-to-all-start.1 = ((bf16[32,512,128]{2,1,0:T(8,128)(2,1)}), bf16[32,512,128]{2,1,0:T(8,128)(2,1)}, u32[]{:S(2)}, u32[]{:S(2)}) async-start(bf16[32,512,128]{2,1,0:T(8,128)(2,1)} %broadcast_select_fusion), calls=%async_computation.1 | async-start | bytes 8388608 | tf_op jit(solution)/shard_map/all_to_all | solution.py:51
  95.3 229.1 %all-gather.3.cloned.1.call-start = ((), (), s32[]{:S(2)}) async-start(), calls=%async_computation.2 | async-start | bytes 1081344 | tf_op jit(solution)/shard_map/all_gather | solution.py:46
  321.1 3.3 copy-start.3
  324.4 157.5 %copy-start.5 = (s32[1,1,128]{2,1,0:T(1,128)S(1)}, s32[1,1,128]{2,1,0:T(1,128)}, u32[]{:S(2)}) copy-start(s32[1,1,128]{2,1,0:T(1,128)} %param.20) | copy-start | bytes 1540
Sparse Core Ops, SparseCore 0:
  98.4 67.9 all-gather.2
where the time goes:
time: 526 us; the launch traced here: 521 us
  local copies, waits for them, and re-layouts  135 us (26%)
  other arithmetic  132 us (25%)
  matrix products  110 us (21%)
  waiting for transfers between devices  52 us (10%)
  blocking collectives  41 us (8%)
  loops' own time  31.8 us (6%)
  between operations  14.7 us (3%)
    dot_general x16, matrix products, query_block_scores(): jnp.einsum('qtd,pdj->qtpj', query_tile_rows, embeds, preferred_element_ty...  110 us
    reduce_sum x1, other arithmetic, decode_shard(): jnp.sum(summed * summed, axis=1, keepdims=True) + EPS  109 us
    gather x2, local copies, waits for them, and re-layouts, decode_shard(): jnp.take(tablevec, token_refs, axis=0)  64 us
    gather x1, local copies, waits for them, and re-layouts, local(): jnp.take(centroids, lax.all_to_all(wanted, 'cent', split_axis=0, concat_a...  59.4 us
    all_to_all x1, waiting for transfers between devices, local(): lax.all_to_all(fetched, 'cent', split_axis=0, concat_axis=0, tiled=True)  51.4 us
    another operation x1, loops' own time, local(): lax.map(query_block_scores, block_starts).reshape(qcount, passage_count)  31.8 us
    all_gather x1, blocking collectives, local(): all_tops = lax.all_gather(local_tops[None], 'cent', axis=0, tiled=True)  25 us
    all_to_all x1, blocking collectives, local(): lax.all_to_all(wanted, 'cent', split_axis=0, concat_axis=0, tiled=True)  16 us
  transfers between devices with their start and end apart: 2, of which 1 were waited for; matrix products, arithmetic and copies ran while one was open for 34% of the time, Pallas kernels for 0%

commit v1 on v0

v1 whole, which is shorter than its diff:
```python
import jax
import jax.numpy as jnp
from jax import lax
from jax.experimental import pallas as pl
from jax.experimental.pallas import tpu as pltpu
from jax.sharding import PartitionSpec as P

TOPK = 100
NEG = -1e30
EPS = 1e-6
LOW = float("-inf")
TB = 16
CHUNK = 256
LAG = 3
MESH = pl.DeviceIdType.MESH


def fetch_kernel(
    cent_hbm, wanted, own, tab, qall,
    stage, cent, asked, asked_s, gath, sbuf,
    stage_sem, local_sem, off_send, off_recv, q_send, q_recv, blk_send, blk_recv,
    left_send, right_send, left_recv, right_recv, left_relay, right_relay,
):
    me, z = lax.axis_index("cent"), lax.axis_index("qry")
    n, nz = lax.axis_size("cent"), lax.axis_size("qry")
    right, left = lax.rem(z + 1, nz), lax.rem(z + nz - 1, nz)
    rows = wanted.shape[2]
    pieces = cent_hbm.shape[0] // stage.shape[1]
    depth = stage.shape[1]

    def load(i):
        return pltpu.make_async_copy(
            cent_hbm.at[pl.ds(pl.multiple_of(i * depth, depth), depth)],
            stage.at[lax.rem(i, 2)],
            stage_sem.at[lax.rem(i, 2)],
        )

    load(0).start()
    load(1).start()

    barrier = pltpu.get_barrier_semaphore()

    @pl.loop(1, n)
    def _(i):
        pl.semaphore_signal(barrier, inc=1, device_id=(lax.rem(me + i, n), z), device_id_type=MESH)

    for side in (left, right):
        pl.semaphore_signal(barrier, inc=1, device_id=(me, side), device_id_type=MESH)
    pl.semaphore_wait(barrier, n + 1)

    @pl.loop(1, n)
    def _(i):
        peer = lax.rem(me + i, n)
        pltpu.make_async_remote_copy(
            src_ref=wanted.at[peer], dst_ref=asked.at[me], send_sem=off_send, recv_sem=off_recv,
            device_id=(peer, z), device_id_type=MESH,
        ).start()

    asked[me] = wanted[me]
    qall[me] = own[...]

    @pl.loop(0, pieces)
    def _(i):
        load(i).wait()
        at = pl.multiple_of(i * depth, depth)
        slot = lax.rem(i, 2)

        @pl.loop(0, depth // 256)
        def _(j):
            inner = pl.multiple_of(j * 256, 256)
            cent[pl.ds(at + inner, 256), :] = stage[slot, pl.ds(inner, 256), :].astype(jnp.float32)

        @pl.when(i + 2 < pieces)
        def _():
            load(i + 2).start()

    offsets = pltpu.make_async_remote_copy(
        src_ref=wanted.at[pl.ds(0, n - 1)], dst_ref=asked.at[pl.ds(0, n - 1)],
        send_sem=off_send, recv_sem=off_recv, device_id=(lax.rem(me + 1, n), z), device_id_type=MESH,
    )
    offsets.wait_recv()
    to_scalar = pltpu.make_async_copy(asked, asked_s, local_sem)
    to_scalar.start()
    to_scalar.wait()

    def block_copy(i):
        peer = lax.rem(me + i, n)
        return pltpu.make_async_remote_copy(
            src_ref=sbuf.at[i], dst_ref=tab.at[me, z], send_sem=blk_send, recv_sem=blk_recv.at[i],
            device_id=(peer, z), device_id_type=MESH,
        )

    def along(owner, quarter, side, send, recv):
        return pltpu.make_async_remote_copy(
            src_ref=tab.at[owner, quarter], dst_ref=tab.at[owner, quarter], send_sem=send, recv_sem=recv,
            device_id=(me, side), device_id_type=MESH,
        )

    @pl.loop(0, n + 2 * LAG)
    def _(i):
        @pl.when(i < n)
        def _():
            peer = lax.rem(me + i, n)
            for r in range(rows):
                gath[r : r + 1, :] = cent[pl.ds(asked_s[peer, 0, r], 1), :]

            @pl.when(i == 0)
            def _():
                tab[me, z] = gath[...].astype(jnp.bfloat16)

            @pl.when(i > 0)
            def _():
                sbuf[i] = gath[...].astype(jnp.bfloat16)
                block_copy(i).start()
                pltpu.make_async_remote_copy(
                    src_ref=own, dst_ref=qall.at[me], send_sem=q_send, recv_sem=q_recv,
                    device_id=(peer, z), device_id_type=MESH,
                ).start()

        @pl.when((i >= LAG) & (i < n + LAG))
        def _():
            k = i - LAG
            owner = lax.rem(me + n - k, n)

            @pl.when(k > 0)
            def _():
                block_copy(k).wait_recv()

            along(owner, z, right, right_send, left_recv.at[k]).start()
            along(owner, z, left, left_send, right_recv.at[k]).start()

        @pl.when(i >= 2 * LAG)
        def _():
            k = i - 2 * LAG
            owner = lax.rem(me + n - k, n)
            along(owner, left, right, right_send, left_recv.at[k]).wait_recv()
            along(owner, right, left, left_send, right_recv.at[k]).wait_recv()

            @pl.when(lax.rem(k, 2) == 0)
            def _():
                along(owner, left, right, right_send, left_relay).start()

            @pl.when(lax.rem(k, 2) == 1)
            def _():
                along(owner, right, left, left_send, right_relay).start()

    def bulk(ref, send, recv):
        return pltpu.make_async_remote_copy(
            src_ref=ref, dst_ref=ref, send_sem=send, recv_sem=recv, device_id=(me, right), device_id_type=MESH,
        )

    half = tab.at[pl.ds(0, n // 2 // nz)]
    bulk(half, right_send, left_relay).wait_recv()
    bulk(half, right_send, right_relay).wait_recv()
    bulk(qall.at[pl.ds(0, n - 1)], q_send, q_recv).wait()
    offsets.wait_send()
    bulk(sbuf.at[pl.ds(0, n - 1)], blk_send, q_recv).wait_send()
    sent = tab.at[pl.ds(0, (n + n // 2) // nz)]
    bulk(sent, right_send, left_relay).wait_send()
    bulk(sent, left_send, left_relay).wait_send()


def fetch(centroids, wanted, own):
    n, nz = lax.axis_size("cent"), lax.axis_size("qry")
    rows = wanted.shape[2]
    vmem = pl.BlockSpec(memory_space=pltpu.VMEM)
    dma = pltpu.SemaphoreType.DMA
    return pl.pallas_call(
        fetch_kernel,
        out_shape=(
            jax.ShapeDtypeStruct((n, nz, rows, 128), jnp.bfloat16),
            jax.ShapeDtypeStruct((n,) + own.shape, jnp.bfloat16),
        ),
        in_specs=[pl.BlockSpec(memory_space=pl.ANY), vmem, vmem],
        out_specs=(vmem, vmem),
        scratch_shapes=[
            pltpu.VMEM((2, 4096, 128), jnp.bfloat16),
            pltpu.VMEM(centroids.shape, jnp.float32),
            pltpu.VMEM((n, 1, rows), jnp.int32),
            pltpu.SMEM((n, 1, rows), jnp.int32),
            pltpu.VMEM((rows, 128), jnp.float32),
            pltpu.VMEM((n, rows, 128), jnp.bfloat16),
            dma((2,)), dma, dma, dma, dma, dma, dma, dma((n,)),
            dma, dma, dma((n,)), dma((n,)), dma, dma,
        ],
        compiler_params=pltpu.CompilerParams(
            collective_id=0, has_side_effects=True, vmem_limit_bytes=56 * 2**20
        ),
    )(centroids, wanted, own)


def merge_kernel(tops, shard_out, best_out, outbox, inbox, send_sem, recv_sem):
    me, z = lax.axis_index("cent"), lax.axis_index("qry")
    n = lax.axis_size("cent")
    per = outbox.shape[1]
    keep = shard_out.shape[2]

    barrier = pltpu.get_barrier_semaphore()

    @pl.loop(1, n)
    def _(i):
        pl.semaphore_signal(barrier, inc=1, device_id=(lax.rem(me + i, n), z), device_id_type=MESH)

    for i in range(tops.shape[0] // per):
        outbox[i] = tops[i * per : (i + 1) * per, :]
    inbox[me] = outbox[me]
    pl.semaphore_wait(barrier, n - 1)

    @pl.loop(1, n)
    def _(i):
        peer = lax.rem(me + i, n)
        pltpu.make_async_remote_copy(
            src_ref=outbox.at[peer], dst_ref=inbox.at[me], send_sem=send_sem, recv_sem=recv_sem,
            device_id=(peer, z), device_id_type=MESH,
        ).start()

    pltpu.make_async_remote_copy(
        src_ref=outbox.at[pl.ds(0, n - 1)], dst_ref=inbox.at[pl.ds(0, n - 1)],
        send_sem=send_sem, recv_sem=recv_sem, device_id=(lax.rem(me + 1, n), z), device_id_type=MESH,
    ).wait()

    lists = [inbox[:, q, :] for q in range(per)]
    for q in range(per):
        shard_out[q] = lists[q][:, :keep]
    column = jnp.concatenate(lists, axis=0)
    across = column.T
    width = per * n
    row = across[0:16, :]
    lane = lax.broadcasted_iota(jnp.int32, (16, width), 1)
    shard = lax.rem(lane, n)
    place = lax.broadcasted_iota(jnp.int32, (16, width), 0)

    def count(r, rank):
        near = pltpu.roll(row, r, 1)
        far = pltpu.roll(row, r + width - n, 1)
        other = jnp.where(shard >= r, near, far)
        wrapped = shard < r
        for k in range(keep):
            rival = other[k : k + 1, :]
            ahead = (rival > row) | ((rival == row) & ~wrapped)
            rank = rank + ahead.astype(jnp.int32)
        return rank

    rank = lax.fori_loop(1, n, count, place)
    ranks = jnp.concatenate([rank, jnp.zeros((width - 16, width), jnp.int32)], axis=0).T
    target = lax.broadcasted_iota(jnp.int32, (width, 128), 1)
    found = jnp.zeros((width, 128), jnp.float32)
    for k in range(keep):
        found = found + jnp.where(ranks[:, k : k + 1] == target, column[:, k : k + 1], 0.0)
    for q in range(per):
        best = jnp.sum(found[q * n : (q + 1) * n, :], axis=0, keepdims=True)
        best_out[q : q + 1, :] = best[:, :TOPK]


def merge(tops, per, keep):
    n = lax.axis_size("cent")
    vmem = pl.BlockSpec(memory_space=pltpu.VMEM)
    return pl.pallas_call(
        merge_kernel,
        out_shape=(
            jax.ShapeDtypeStruct((per, n, keep), jnp.float32),
            jax.ShapeDtypeStruct((per, TOPK), jnp.float32),
        ),
        in_specs=[vmem],
        out_specs=(vmem, vmem),
        scratch_shapes=[
            pltpu.VMEM((n, per, 128), jnp.float32),
            pltpu.VMEM((n, per, 128), jnp.float32),
            pltpu.SemaphoreType.DMA,
            pltpu.SemaphoreType.DMA,
        ],
        compiler_params=pltpu.CompilerParams(collective_id=1, has_side_effects=True),
    )(tops)


def score_kernel(
    refs, perm, lens, packed_ref, bv_ref, len_ref, table_ref, q_ref, cand_ref, live_ref,
    out_ref, tab, resid, gath, first, acc, scores, blk_g, blk_b,
):
    passages = packed_ref.shape[0]
    groups = passages // 8
    columns = q_ref.shape[1]
    queries = cand_ref.shape[1]
    slots = cand_ref.shape[0]
    ptok = packed_ref.shape[2]
    rows = TB * 8

    @pl.loop(0, table_ref.shape[0] // 512)
    def _(i):
        at = pl.ds(pl.multiple_of(i * 512, 512), 512)
        tab[at, :] = table_ref[at, :].astype(jnp.float32)

    @pl.loop(0, passages)
    def _(i):
        words = packed_ref[perm[i]]
        digits = jnp.concatenate([(words >> (2 * k)) & 3 for k in range(8)], axis=0)
        low = jnp.where(digits == 0, bv_ref[0], bv_ref[1])
        high = jnp.where(digits == 2, bv_ref[2], bv_ref[3])
        value = jnp.where(digits < 2, low, high)
        base = lax.div(i, 8) * (8 * ptok) + lax.rem(i, 8)
        resid[pl.ds(base, ptok, stride=8), :] = value.T

    acc[...] = jnp.full(acc.shape, LOW, jnp.float32)

    def add_group(g, n):
        count = lax.div(lens[g * 8] + (TB - 1), TB)

        def add(b, m):
            blk_g[m] = g
            blk_b[m] = b
            return m + 1

        return lax.fori_loop(0, count, add, n)

    total = lax.fori_loop(0, groups, add_group, 0)

    def embed(i):
        g, b = blk_g[i], blk_b[i]
        where = [perm[g * 8 + p] * ptok + b * TB for p in range(8)]
        for t in range(TB):
            for p in range(8):
                gath[pl.ds(t * 8 + p, 1), :] = tab[pl.ds(refs[where[p] + t], 1), :]
        start = pl.multiple_of(g * (8 * ptok) + b * rows, rows)
        summed = gath[...] + resid[pl.ds(start, rows), :]
        norm = jnp.sum(summed * summed, axis=1, keepdims=True)
        unit = (summed * lax.rsqrt(norm + EPS)).reshape(TB, 8, 128)
        head = jnp.where(b == 0, unit[0], first[...])
        first[...] = head
        token = b * TB + lax.broadcasted_iota(jnp.int32, (TB, 8, 128), 0)
        unit = jnp.where(token < len_ref[g][None], unit, head[None])
        return unit.reshape(rows, 128).astype(jnp.bfloat16)

    def step(i, unit):
        g = blk_g[i]
        following = embed(jnp.minimum(i + 1, total - 1))
        for c in range(0, columns, CHUNK):
            sim = jnp.dot(unit, q_ref[:, c : c + CHUNK], preferred_element_type=jnp.float32)
            best = jnp.max(sim.reshape(TB, 8, CHUNK), axis=0)
            acc[g, :, c : c + CHUNK] = jnp.maximum(acc[g, :, c : c + CHUNK], best)
        return following

    lax.fori_loop(0, total, step, embed(0))

    @pl.loop(0, groups)
    def _(g):
        total_sum = acc[g, :, 0:queries]
        for t in range(1, columns // queries):
            total_sum = total_sum + acc[g, :, t * queries : (t + 1) * queries]
        scores[pl.ds(pl.multiple_of(g * 8, 8), 8), :] = total_sum

    cand = cand_ref[...]

    def pick(r, picked):
        return jnp.where(cand == perm[r], scores[pl.ds(r, 1), :], picked)

    picked = lax.fori_loop(0, passages, pick, jnp.zeros((slots, queries), jnp.float32), unroll=8)
    place = lax.broadcasted_iota(jnp.int32, (slots, queries), 0)
    values = jnp.where(place < live_ref[...], picked, NEG)
    place_out = lax.broadcasted_iota(jnp.int32, (16, queries), 0)
    tops = jnp.zeros((16, queries), jnp.float32)
    for k in range(slots // 4):
        top = jnp.max(values, axis=0, keepdims=True)
        tops = jnp.where(place_out == k, top, tops)
        at = jnp.min(jnp.where(values == top, place, slots), axis=0, keepdims=True)
        values = jnp.where(place == at, LOW, values)
    padded = jnp.concatenate([tops, jnp.zeros((128 - 16, queries), jnp.float32)], axis=0)
    out_ref[...] = padded.T


def local_scores(table, refs, packed, lengths, bucket_values, qcols, cand, live):
    passages, _, ptok = packed.shape
    queries, slots = cand.shape
    perm = jnp.argsort(-lengths).astype(jnp.int32)
    lens = lengths[perm]
    len_rows = jnp.broadcast_to(lens.reshape(passages // 8, 8, 1), (passages // 8, 8, 128))
    bv = jnp.broadcast_to(bucket_values[:, :, None], (4, 128, ptok))
    vmem = pl.BlockSpec(memory_space=pltpu.VMEM)
    smem = pl.BlockSpec(memory_space=pltpu.SMEM)
    blocks = passages // 8 * (ptok // TB)
    return pl.pallas_call(
        score_kernel,
        out_shape=jax.ShapeDtypeStruct((queries, 128), jnp.float32),
        in_specs=[smem, smem, smem, vmem, vmem, vmem, vmem, vmem, vmem, vmem],
        out_specs=vmem,
        scratch_shapes=[
            pltpu.VMEM((table.shape[0], 128), jnp.float32),
            pltpu.VMEM((passages * ptok, 128), jnp.float32),
            pltpu.VMEM((TB * 8, 128), jnp.float32),
            pltpu.VMEM((8, 128), jnp.float32),
            pltpu.VMEM((passages // 8, 8, qcols.shape[1]), jnp.float32),
            pltpu.VMEM((passages, queries), jnp.float32),
            pltpu.SMEM((blocks,), jnp.int32),
            pltpu.SMEM((blocks,), jnp.int32),
        ],
        compiler_params=pltpu.CompilerParams(vmem_limit_bytes=56 * 2**20),
    )(refs.reshape(-1), perm, lens, packed, bv, len_rows, table, qcols, cand.T, live[None, :])


def local(
    queries,
    centroids,
    shard_table,
    token_refs,
    packed_residual_buckets,
    passage_lengths,
    bucket_values,
    candidates,
    live_counts,
):
    n, nz = lax.axis_size("cent"), lax.axis_size("qry")
    per, tokens, width = queries.shape[1:]
    by_owner = shard_table.reshape(n, nz, -1)
    wanted = lax.dynamic_slice_in_dim(by_owner, lax.axis_index("qry"), 1, 1)
    table, everyone = fetch(centroids, wanted, queries.reshape(per * tokens, width))
    qcols = jnp.transpose(everyone.reshape(n * per, tokens, width), (2, 1, 0)).reshape(width, -1)
    tops = local_scores(
        table.reshape(-1, width), token_refs, packed_residual_buckets, passage_lengths, bucket_values, qcols,
        candidates[0, 0], live_counts[0, 0],
    )
    shard_tops, best_scores = merge(tops, per, candidates.shape[3] // 4)
    return (shard_tops[None], best_scores[None])


def solution(mesh):
    return jax.shard_map(
        local,
        mesh=mesh,
        in_specs=(
            P("qry", "cent", None, None),
            P("cent", None),
            P("cent", None),
            P("cent", None),
            P("cent", None, None),
            P("cent"),
            P(),
            P("qry", "cent", None, None),
            P("qry", "cent", None),
        ),
        out_specs=(P("qry", "cent", None, None), P("qry", "cent", None)),
        check_vma=False,
    )
```

time: 526 us -> 153 us (0.29)
  Pallas kernels: 0 us -> 139 us
  other arithmetic: 132 us -> 2.55 us
  local copies, waits for them, and re-layouts: 135 us -> 11 us
  matrix products: 110 us -> 0 us
  waiting for transfers between devices: 52 us -> 0 us
  blocking collectives: 41 us -> 0 us
  loops' own time: 31.8 us -> 0 us
  between operations: 14.7 us -> 0.71 us
    pallas_call x0 -> x3, Pallas kernels: none -> 139 us  [the longest x1 69.3 us: fetch(): pl.pallas_call(fetch_kernel, out_shape=(jax.ShapeDtypeStruct((n, nz, rows...]
    gather x3 -> x1, local copies, waits for them, and re-layouts: 123 us -> 1.23 us  [local_scores(): lens = lengths[perm]]
    reduce_sum x18 -> x0, other arithmetic: 114 us -> none  [the longest x1 109 us: decode_shard(): jnp.sum(summed * summed, axis=1, keepdims=True) + EPS]
    dot_general x16 -> x0, matrix products: 110 us -> none  [query_block_scores(): jnp.einsum('qtd,pdj->qtpj', query_tile_rows, embeds, preferred_element_ty...]
    all_to_all x1 -> x0, waiting for transfers between devices: 51.4 us -> none  [local(): lax.all_to_all(fetched, 'cent', split_axis=0, concat_axis=0, tiled=True)]
    another operation x1 -> x0, loops' own time: 31.8 us -> none  [local(): lax.map(query_block_scores, block_starts).reshape(qcount, passage_count)]
    all_gather x1 -> x0, blocking collectives: 25 us -> none  [local(): all_tops = lax.all_gather(local_tops[None], 'cent', axis=0, tiled=True)]
    all_to_all x1 -> x0, blocking collectives: 16 us -> none  [local(): lax.all_to_all(wanted, 'cent', split_axis=0, concat_axis=0, tiled=True)]
  transfers between devices with their start and end apart: 2 -> 0, of which waited for: 1 -> 0; matrix products, arithmetic and copies ran while one was open for 34% -> 0% of each run, Pallas kernels for 0% -> 0%
where the time goes in v1:
time: 153 us
  Pallas kernels  139 us (91%)
  local copies, waits for them, and re-layouts  11 us (7%)
  other arithmetic  2.55 us (2%)
    pallas_call x1, Pallas kernels, fetch(): pl.pallas_call(fetch_kernel, out_shape=(jax.ShapeDtypeStruct((n, nz, rows...  69.3 us
    pallas_call x1, Pallas kernels, local_scores(): pl.pallas_call(score_kernel, out_shape=jax.ShapeDtypeStruct((queries, 128...  56.8 us
    pallas_call x1, Pallas kernels, merge(): pl.pallas_call(merge_kernel, out_shape=(jax.ShapeDtypeStruct((per, n, kee...  12.6 us
    unnamed x13, local copies, waits for them, and re-layouts  5.02 us

profile of v1, /device:TPU:1, one launch (start us, length us, event | category | flops | bytes accessed | tf_op | source)
XLA Modules:
  0.0 152.9 jit_solution(8967610587584070147)
XLA Ops:
  0.6 0.0 copy-start
  0.6 0.0 copy-start.1
  0.7 0.0 copy-start.3
  0.7 0.8 copy-done
  1.5 0.6 constant_dynamic-slice_fusion.wanted
  2.1 69.3 %shard_map.104 = (bf16[32,4,128,128]{3,2,1,0:T(8,128)(2,1)}, bf16[32,128,128]{2,1,0:T(8,128)(2,1)}) custom-call(bf16[32768,128]{1,0:T(8,128)(2,1)} %cent_hbm.1, s32[32,1,128]{2,1,0:T(1,128)} %constant_dynamic-slice_fusion.wanted, bf16[128,128]{1,0:T(8,128)(2,1)} %bitcast.23), custom_call_target="tpu_custom_call" | custom-call | tf_op jit(solution)/shard_map/pallas_call | solution.py:168
  71.4 2.5 %copy.13 = bf16[128,32,128]{0,1,2:T(8,128)(2,1)S(1)} copy(bf16[128,32,128]{2,1,0:T(8,128)(2,1)} %bitcast.20) | data formatting | bytes 2097152 | tf_op jit(solution)/shard_map/reshape | solution.py:415
  73.9 1.4 copy.17
  75.3 0.0 copy-done.1
  75.3 2.5 %sort.17 = (s32[128]{0:T(128)}, s32[128]{0:T(128)S(1)}) sort(s32[128]{0:T(128)S(1)} %neg.3, s32[128]{0:T(128)S(1)} %iota.4), dimensions={0}, to_apply=%region_0.0 | sort | flops 896 | bytes 2048 | tf_op jit(solution)/shard_map/jit(argsort)/sort | solution.py:373
  77.9 0.0 copy-start.4
  77.9 1.2 gather_fusion
  79.1 0.0 copy-start.2
  79.1 0.1 broadcast_in_dim.24
  79.2 0.7 broadcast_in_dim.25.len_ref
  79.9 0.0 copy-done.3
  79.9 0.8 broadcast_in_dim.23.bv_ref
  80.7 0.0 copy-done.4
  80.7 0.0 copy-done.2
  80.8 56.8 %shard_map.105.tops = f32[128,128]{1,0:T(8,128)} custom-call(s32[16384]{0:T(1024)} %bitcast.21, s32[128]{0:T(128)} %copy-done.4, s32[128]{0:T(128)} %copy-done.2, s32[128,16,128]{2,1,0:T(8,128)} %packed_ref.1, f32[4,128,128]{2,1,0:T(8,128)} %broadcast_in_dim.23.bv_ref, s32[16,8,128]{2,1,0:T(8,128)} %broadcast_in_dim.25.len_ref, bf16[16384,128]{1,0:T(8,128)(2,1)} %bitcast.17, ...), custom_call_target="tpu_custom_call" | custom-call | tf_op jit(solution)/shard_map/pallas_call | solution.py:380
  137.5 12.6 %shard_map.106 = (f32[4,32,12]{2,1,0:T(8,128)}, f32[4,100]{1,0:T(4,128)}) custom-call(f32[128,128]{1,0:T(8,128)} %shard_map.105.tops), custom_call_target="tpu_custom_call" | custom-call | tf_op jit(solution)/shard_map/pallas_call | solution.py:258
  150.1 1.5 %copy.14 = f32[1,4,32,12]{2,1,3,0:T(4,128)} copy(f32[1,4,32,12]{3,2,1,0:T(8,128)} %bitcast.22) | data formatting | bytes 12288
  151.7 1.2 copy.19
  (4 shorter events, 0.0 us)
Async XLA Ops:
  0.6 0.8 copy-start
  0.6 74.7 %copy-start.1 = (s32[128]{0:T(128)S(1)}, s32[128]{0:T(128)}, u32[]{:S(2)}) copy-start(s32[128]{0:T(128)} %param.14) | copy-start | bytes 1540
  0.7 79.2 %copy-start.3 = (f32[4,128]{1,0:T(4,128)S(1)}, f32[4,128]{1,0:T(4,128)}, u32[]{:S(2)}) copy-start(f32[4,128]{1,0:T(4,128)} %param.15) | copy-start | bytes 6148
  77.9 2.9 %copy-start.4 = (s32[128]{0:T(128)}, s32[128]{0:T(128)S(1)}, u32[]{:S(2)}) copy-start(s32[128]{0:T(128)S(1)} %get-tuple-element.7.perm) | copy-start | bytes 1540
  79.1 1.7 %copy-start.2 = (s32[128]{0:T(128)}, s32[128]{0:T(128)S(1)}, u32[]{:S(2)}) copy-start(s32[128]{0:T(128)S(1)} %gather_fusion) | copy-start | bytes 1540

commit v2 on v0

v2 whole, which is shorter than its diff:
```python
import jax
import jax.numpy as jnp
from jax import lax
from jax.experimental import pallas as pl
from jax.experimental.pallas import tpu as pltpu
from jax.sharding import PartitionSpec as P

TOPK = 100
NEG = -1e30
EPS = 1e-6
LOW = float("-inf")
TB = 16
CHUNK = 512
UNIT = 4
MESH = pl.DeviceIdType.MESH


def fetch_kernel(
    cent_hbm, wanted, own, lengths, packed, buckets, tab, resid_hbm, qcols, order,
    stage, cent, asked, asked_s, sbuf, qall, qwide, spread, resid, order_s,
    stage_sem, asked_sem, order_sem, own_sem, resid_sem, off_send, off_recv,
    q_send, q_recv, pair_send, pair_recv, blk_send, blk_recv, half_recv, z_send, left_recv, right_recv, far_recv,
):
    me, z = lax.axis_index("cent"), lax.axis_index("qry")
    n, nz = lax.axis_size("cent"), lax.axis_size("qry")
    core = lax.rem(me, 2)
    chip = lax.div(me, 2)
    chips = n // 2
    right, far, left = lax.rem(z + 1, nz), lax.rem(z + 2, nz), lax.rem(z + 3, nz)
    rows = tab.shape[2]
    part = sbuf.shape[1] - rows
    pieces = stage_sem.shape[0]
    depth = stage.shape[0] // pieces
    passages = packed.shape[0]
    ptok = packed.shape[2]

    loads = [
        pltpu.make_async_copy(
            cent_hbm.at[i * depth : (i + 1) * depth], stage.at[i * depth : (i + 1) * depth], stage_sem.at[i]
        )
        for i in range(pieces)
    ]
    for load in loads:
        load.start()

    barrier = pltpu.get_barrier_semaphore()

    @pl.loop(1, n)
    def _(i):
        pl.semaphore_signal(barrier, inc=1, device_id=(lax.rem(me + i, n), z), device_id_type=MESH)

    for side in (left, right, far):
        pl.semaphore_signal(barrier, inc=1, device_id=(me, side), device_id_type=MESH)

    across = jnp.broadcast_to(lengths[...], (passages, passages))
    down = across.T
    line = lax.broadcasted_iota(jnp.int32, (passages, passages), 0)
    lane = lax.broadcasted_iota(jnp.int32, (passages, passages), 1)
    ahead = (down > across) | ((down == across) & (line < lane))
    rank = jnp.sum(ahead.astype(jnp.int32), axis=0, keepdims=True)
    hit = jnp.broadcast_to(rank, (passages, passages)).T == lane
    order[0:1, :] = jnp.sum(jnp.where(hit, line, 0), axis=0, keepdims=True)
    order[1:2, :] = jnp.sum(jnp.where(hit, down, 0), axis=0, keepdims=True)
    order[2:8, :] = jnp.zeros((6, passages), jnp.int32)
    to_order = pltpu.make_async_copy(order, order_s, order_sem)
    to_order.start()
    for b in range(4):
        spread[b] = jnp.broadcast_to(buckets[b : b + 1, :], (ptok, 128)).T

    def widen(first, last):
        for i in range(first, last):
            loads[i].wait()

            @pl.loop(0, depth // 512)
            def _(j):
                at = pl.ds(pl.multiple_of(i * depth + j * 512, 512), 512)
                cent[at, :] = stage[at, :].astype(jnp.float32)

    widen(0, pieces // 2)
    pl.semaphore_wait(barrier, n + 2)

    @pl.loop(1, n)
    def _(i):
        peer = lax.rem(me + i, n)
        pltpu.make_async_remote_copy(
            src_ref=wanted.at[peer], dst_ref=asked.at[me], send_sem=off_send, recv_sem=off_recv,
            device_id=(peer, z), device_id_type=MESH,
        ).start()

    asked[me] = wanted[me]
    qall[chip, core] = own[...]
    widen(pieces // 2, pieces)
    to_order.wait()

    offsets = pltpu.make_async_remote_copy(
        src_ref=wanted.at[pl.ds(0, n - 1)], dst_ref=asked.at[pl.ds(0, n - 1)],
        send_sem=off_send, recv_sem=off_recv, device_id=(lax.rem(me + 1, n), z), device_id_type=MESH,
    )
    offsets.wait_recv()
    to_scalar = pltpu.make_async_copy(asked, asked_s, asked_sem)
    to_scalar.start()
    to_scalar.wait()

    sub = lax.broadcasted_iota(jnp.int32, (16, 128), 0)

    def pull(i, line, start, count):
        peer = lax.rem(me + i, n)
        for r in range(0, count, 16):
            tile = jnp.broadcast_to(cent[pl.ds(asked_s[peer, line, r], 1), :], (16, 128))
            for k in range(1, 16):
                value = jnp.broadcast_to(cent[pl.ds(asked_s[peer, line, r + k], 1), :], (16, 128))
                tile = jnp.where(sub == k, value, tile)
            sbuf[i, start + r : start + r + 16, :] = tile.astype(jnp.bfloat16)

    def block_copy(i):
        return pltpu.make_async_remote_copy(
            src_ref=sbuf.at[i, pl.ds(0, rows)], dst_ref=tab.at[me, z], send_sem=blk_send, recv_sem=blk_recv.at[i],
            device_id=(lax.rem(me + i, n), z), device_id_type=MESH,
        )

    pull(0, 0, 0, rows)
    keep_own = pltpu.make_async_copy(sbuf.at[0, pl.ds(0, rows)], tab.at[me, z], own_sem.at[0])
    keep_own.start()

    @pl.loop(1, n)
    def _(i):
        pull(i, 0, 0, rows)
        block_copy(i).start()

    def along(ref, side, recv):
        return pltpu.make_async_remote_copy(
            src_ref=ref, dst_ref=ref, send_sem=z_send, recv_sem=recv, device_id=(me, side), device_id_type=MESH,
        )

    def forward(k):
        owner = lax.rem(me + n - k, n)
        along(tab.at[owner, z], right, left_recv).start()
        along(tab.at[owner, z], left, right_recv).start()
        along(tab.at[owner, z, pl.ds(part, rows - part)], far, far_recv).start()

    def decode(i):
        words = packed[order_s[0, i]]
        digits = jnp.concatenate([(words >> (2 * k)) & 3 for k in range(8)], axis=0)
        low = jnp.where(digits == 0, spread[0], spread[1])
        high = jnp.where(digits == 2, spread[2], spread[3])
        value = jnp.where(digits < 2, low, high)
        resid[lax.div(i, 8), pl.ds(lax.rem(i, 8), ptok, stride=8), :] = value.T

    def extras(k):
        for j in range(passages // n):
            decode(k * (passages // n) + j)
        pull(k, 1, rows, part)

    def save(g):
        return pltpu.make_async_copy(resid.at[g], resid_hbm.at[g], resid_sem)

    keep_own.wait()
    forward(0)
    extras(0)
    keep_half = pltpu.make_async_copy(sbuf.at[0, pl.ds(rows, part)], tab.at[me, far, pl.ds(0, part)], own_sem.at[1])
    keep_half.start()

    @pl.loop(1, n)
    def _(k):
        block_copy(k).wait_recv()
        forward(k)
        extras(k)
        pltpu.make_async_remote_copy(
            src_ref=sbuf.at[k, pl.ds(rows, part)], dst_ref=tab.at[me, far, pl.ds(0, part)],
            send_sem=blk_send, recv_sem=half_recv,
            device_id=(lax.rem(me + k, n), z), device_id_type=MESH,
        ).start()

        @pl.when(lax.rem(k, 2) == 0)
        def _():
            pltpu.make_async_remote_copy(
                src_ref=own, dst_ref=qall.at[chip, core], send_sem=q_send, recv_sem=q_recv,
                device_id=(lax.rem(me + k, n), z), device_id_type=MESH,
            ).start()

        @pl.when(lax.rem(k, 2) == 1)
        def _():
            save(lax.div(k, 2)).start()

    def bulk(ref, send, recv):
        return pltpu.make_async_remote_copy(
            src_ref=ref, dst_ref=ref, send_sem=send, recv_sem=recv, device_id=(me, right), device_id_type=MESH,
        )

    bulk(qall.at[pl.ds(0, chips - 1), 0], q_send, q_recv).wait_recv()
    pair = pltpu.make_async_remote_copy(
        src_ref=qall.at[pl.ds(0, chips), core], dst_ref=qall.at[pl.ds(0, chips), core],
        send_sem=pair_send, recv_sem=pair_recv,
        device_id=(me + 1 - 2 * core, z), device_id_type=MESH,
    )
    pair.start()
    pair.wait()

    tokens = own.shape[0] * n // passages
    per = own.shape[0]

    @pl.loop(0, chips)
    def _(i):
        for c in range(2):
            qwide[pl.ds(pl.multiple_of((i * 2 + c) * per, per), per), :] = qall[i, c].astype(jnp.float32)

    for t in range(tokens):
        tile = qwide[pl.ds(t, passages, stride=tokens), :]
        qcols[:, t * passages : (t + 1) * passages] = tile.T.astype(jnp.bfloat16)

    bulk(tab.at[pl.ds(0, n // nz)], z_send, left_recv).wait_recv()
    bulk(tab.at[pl.ds(0, n // nz)], z_send, right_recv).wait_recv()
    bulk(tab.at[pl.ds(0, n), 0, pl.ds(part, rows - part)], z_send, far_recv).wait_recv()
    bulk(sbuf.at[pl.ds(0, n - 1), pl.ds(rows, part)], z_send, half_recv).wait_recv()
    keep_half.wait()
    pltpu.make_async_copy(resid, resid_hbm, resid_sem).wait()
    offsets.wait_send()
    bulk(qall.at[pl.ds(0, chips - 1), 0], q_send, q_recv).wait_send()
    bulk(sbuf.at[pl.ds(0, n - 1)], blk_send, q_recv).wait_send()
    bulk(tab.at[pl.ds(0, 2 * n // nz)], z_send, q_recv).wait_send()
    bulk(tab.at[pl.ds(0, n), 0, pl.ds(part, rows - part)], z_send, q_recv).wait_send()


def fetch(centroids, wanted, own, lengths, packed, buckets):
    n, nz = lax.axis_size("cent"), lax.axis_size("qry")
    rows = wanted.shape[2]
    part = rows // 2
    passages, _, ptok = packed.shape
    vmem = pl.BlockSpec(memory_space=pltpu.VMEM)
    hbm = pl.BlockSpec(memory_space=pl.ANY)
    dma = pltpu.SemaphoreType.DMA
    groups = passages // 8
    return pl.pallas_call(
        fetch_kernel,
        out_shape=(
            jax.ShapeDtypeStruct((n, nz, rows, 128), jnp.bfloat16),
            jax.ShapeDtypeStruct((groups, 8 * ptok, 128), jnp.float32),
            jax.ShapeDtypeStruct((128, n * own.shape[0]), jnp.bfloat16),
            jax.ShapeDtypeStruct((8, passages), jnp.int32),
        ),
        in_specs=[hbm, vmem, vmem, vmem, vmem, vmem],
        out_specs=(hbm, hbm, vmem, vmem),
        scratch_shapes=[
            pltpu.VMEM(centroids.shape, jnp.bfloat16),
            pltpu.VMEM(centroids.shape, jnp.float32),
            pltpu.VMEM((n, 2, rows), jnp.int32),
            pltpu.SMEM((n, 2, rows), jnp.int32),
            pltpu.VMEM((n, rows + part, 128), jnp.bfloat16),
            pltpu.VMEM((n // 2, 2) + own.shape, jnp.bfloat16),
            pltpu.VMEM((n * own.shape[0], 128), jnp.float32),
            pltpu.VMEM((4, 128, ptok), jnp.float32),
            pltpu.VMEM((groups, 8 * ptok, 128), jnp.float32),
            pltpu.SMEM((8, passages), jnp.int32),
            dma((8,)), dma, dma, dma((2,)), dma, dma, dma,
            dma, dma, dma, dma, dma, dma((n,)), dma, dma, dma, dma, dma,
        ],
        compiler_params=pltpu.CompilerParams(
            collective_id=0, has_side_effects=True, vmem_limit_bytes=58 * 2**20
        ),
    )(centroids, wanted, own, lengths, packed, buckets)


def score_kernel(
    refs, order, order_ref, table_hbm, resid_hbm, q_hbm, cand_ref, live_ref,
    out_ref, stage, tab, resid, q_ref, first, acc, scores, len_ref, blk_g, blk_b, stage_sem, resid_sem, q_sem,
):
    passages = order.shape[1]
    groups = passages // 8
    columns = q_ref.shape[1]
    slots, queries = cand_ref.shape
    ptok = resid_hbm.shape[1] // 8
    rows = TB * 8
    pieces = stage_sem.shape[0]
    depth = stage.shape[0] // pieces

    def load(i):
        return pltpu.make_async_copy(
            table_hbm.at[pl.ds(pl.multiple_of(i * depth, depth), depth)],
            stage.at[lax.rem(i, 2)], stage_sem.at[lax.rem(i, 2)],
        )

    loads = [
        pltpu.make_async_copy(
            table_hbm.at[i * depth : (i + 1) * depth], stage.at[i * depth : (i + 1) * depth], stage_sem.at[i]
        )
        for i in range(pieces)
    ]
    for load in loads:
        load.start()
    load_q = pltpu.make_async_copy(q_hbm, q_ref, q_sem)
    load_q.start()

    def load_resid(g):
        return pltpu.make_async_copy(resid_hbm.at[g], resid.at[g], resid_sem.at[g])

    @pl.loop(0, groups)
    def _(g):
        load_resid(g).start()

    acc[...] = jnp.full(acc.shape, LOW, jnp.float32)
    spread = jnp.broadcast_to(order_ref[1:2, :], (passages, passages)).T
    len_ref[...] = spread.reshape(groups, 8, 128)

    def add_group(g, n):
        count = lax.div(order[1, g * 8] + (TB - 1), TB)

        def add(b, m):
            blk_g[m] = g
            blk_b[m] = b
            return m + 1

        return lax.fori_loop(0, count, add, n)

    total = lax.fori_loop(0, groups, add_group, 0)
    for extra in range(UNIT - 1):
        blk_g[total + extra] = blk_g[total - 1]
        blk_b[total + extra] = blk_b[total - 1]
    steps = lax.div(total + (UNIT - 1), UNIT)

    for i, load in enumerate(loads):
        load.wait()

        @pl.loop(0, depth // 512)
        def _(j):
            at = pl.ds(pl.multiple_of(i * depth + j * 512, 512), 512)
            tab[at, :] = stage[at, :].astype(jnp.float32)

    load_q.wait()

    def arrive(first_group, last_group):
        @pl.loop(first_group, last_group + 1)
        def _(g):
            load_resid(g).wait()

    arrive(0, blk_g[UNIT - 1])

    def embed_one(u, i, head):
        g, b = blk_g[i], blk_b[i]
        where = [order[0, g * 8 + p] * ptok + b * TB for p in range(8)]
        sub = lax.broadcasted_iota(jnp.int32, (8, 128), 0)
        tiles = []
        for t in range(TB):
            tile = jnp.broadcast_to(tab[pl.ds(refs[where[0] + t], 1), :], (8, 128))
            for p in range(1, 8):
                tile = jnp.where(sub == p, jnp.broadcast_to(tab[pl.ds(refs[where[p] + t], 1), :], (8, 128)), tile)
            tiles.append(tile)
        got = jnp.concatenate(tiles, axis=0)
        start = pl.multiple_of(b * rows, rows)
        summed = got + resid[g, pl.ds(start, rows), :]
        norm = jnp.sum(summed * summed, axis=1, keepdims=True)
        unit = (summed * lax.rsqrt(norm + EPS)).reshape(TB, 8, 128)
        head = jnp.where(b == 0, unit[0], head)
        token = b * TB + lax.broadcasted_iota(jnp.int32, (TB, 8, 128), 0)
        unit = jnp.where(token < len_ref[g][None], unit, head[None])
        return unit.reshape(rows, 128).astype(jnp.bfloat16), head

    def embed(s):
        head = first[...]
        units = []
        for u in range(UNIT):
            unit, head = embed_one(u, s * UNIT + u, head)
            units.append(unit)
        first[...] = head
        return jnp.concatenate(units, axis=0)

    def step(s, unit):
        later = jnp.minimum(s + 1, steps - 1)
        arrive(blk_g[s * UNIT + UNIT - 1] + 1, blk_g[later * UNIT + UNIT - 1])
        group = [blk_g[s * UNIT + u] for u in range(UNIT)]
        head = first[...]
        following = []
        parts = columns // CHUNK // UNIT
        for part, c in enumerate(range(0, columns, CHUNK)):
            if part % parts == 0:
                u = part // parts
                block, head = embed_one(u, later * UNIT + u, head)
                following.append(block)
            sim = jnp.dot(unit, q_ref[:, c : c + CHUNK], preferred_element_type=jnp.float32)
            best = jnp.max(sim.reshape(UNIT, TB, 8, CHUNK), axis=1)
            for u in range(UNIT):
                acc[group[u], :, c : c + CHUNK] = jnp.maximum(acc[group[u], :, c : c + CHUNK], best[u])
        first[...] = head
        return jnp.concatenate(following, axis=0)

    lax.fori_loop(0, steps, step, embed(0))

    @pl.loop(0, groups)
    def _(g):
        total_sum = acc[g, :, 0:queries]
        for t in range(1, columns // queries):
            total_sum = total_sum + acc[g, :, t * queries : (t + 1) * queries]
        scores[pl.ds(pl.multiple_of(g * 8, 8), 8), :] = total_sum

    cand = cand_ref[...]

    def pick(r, picked):
        return jnp.where(cand == order[0, r], scores[pl.ds(r, 1), :], picked)

    picked = lax.fori_loop(0, passages, pick, jnp.zeros((slots, queries), jnp.float32), unroll=8)
    place = lax.broadcasted_iota(jnp.int32, (slots, queries), 0)
    values = jnp.where(place < live_ref[...], picked, NEG)
    place_out = lax.broadcasted_iota(jnp.int32, (16, queries), 0)
    tops = jnp.zeros((16, queries), jnp.float32)
    for k in range(slots // 4):
        top = jnp.max(values, axis=0, keepdims=True)
        tops = jnp.where(place_out == k, top, tops)
        at = jnp.min(jnp.where(values == top, place, slots), axis=0, keepdims=True)
        values = jnp.where(place == at, LOW, values)
    padded = jnp.concatenate([tops, jnp.zeros((128 - 16, queries), jnp.float32)], axis=0)
    out_ref[...] = padded.T


def score(table, refs, order, resid, qcols, cand, live):
    groups = resid.shape[0]
    passages = order.shape[1]
    queries, slots = cand.shape
    vmem = pl.BlockSpec(memory_space=pltpu.VMEM)
    smem = pl.BlockSpec(memory_space=pltpu.SMEM)
    hbm = pl.BlockSpec(memory_space=pl.ANY)
    blocks = resid.shape[0] * resid.shape[1] // (8 * TB) + UNIT
    return pl.pallas_call(
        score_kernel,
        out_shape=jax.ShapeDtypeStruct((queries, 128), jnp.float32),
        in_specs=[smem, smem, vmem, hbm, hbm, hbm, vmem, vmem],
        out_specs=vmem,
        scratch_shapes=[
            pltpu.VMEM(table.shape, jnp.bfloat16),
            pltpu.VMEM((table.shape[0], 128), jnp.float32),
            pltpu.VMEM(resid.shape, jnp.float32),
            pltpu.VMEM(qcols.shape, jnp.bfloat16),
            pltpu.VMEM((8, 128), jnp.float32),
            pltpu.VMEM((groups, 8, qcols.shape[1]), jnp.float32),
            pltpu.VMEM((passages, queries), jnp.float32),
            pltpu.VMEM((groups, 8, 128), jnp.int32),
            pltpu.SMEM((blocks,), jnp.int32),
            pltpu.SMEM((blocks,), jnp.int32),
            pltpu.SemaphoreType.DMA((8,)),
            pltpu.SemaphoreType.DMA((groups,)),
            pltpu.SemaphoreType.DMA,
        ],
        compiler_params=pltpu.CompilerParams(vmem_limit_bytes=56 * 2**20),
    )(refs.reshape(-1), order, order, table, resid, qcols, cand.T, live[None, :])


def swap_kernel(tops, inbox, outbox, send_sem, recv_sem):
    me, z = lax.axis_index("cent"), lax.axis_index("qry")
    n = lax.axis_size("cent")
    per = outbox.shape[1]
    barrier = pltpu.get_barrier_semaphore()

    @pl.loop(1, n)
    def _(i):
        pl.semaphore_signal(barrier, inc=1, device_id=(lax.rem(me + i, n), z), device_id_type=MESH)

    for i in range(tops.shape[0] // per):
        outbox[i] = tops[i * per : (i + 1) * per, :]
    inbox[me] = outbox[me]
    pl.semaphore_wait(barrier, n - 1)

    @pl.loop(1, n)
    def _(i):
        peer = lax.rem(me + i, n)
        pltpu.make_async_remote_copy(
            src_ref=outbox.at[peer], dst_ref=inbox.at[me], send_sem=send_sem, recv_sem=recv_sem,
            device_id=(peer, z), device_id_type=MESH,
        ).start()

    pltpu.make_async_remote_copy(
        src_ref=outbox.at[pl.ds(0, n - 1)], dst_ref=inbox.at[pl.ds(0, n - 1)],
        send_sem=send_sem, recv_sem=recv_sem, device_id=(lax.rem(me + 1, n), z), device_id_type=MESH,
    ).wait()


def swap(tops, per):
    n = lax.axis_size("cent")
    vmem = pl.BlockSpec(memory_space=pltpu.VMEM)
    return pl.pallas_call(
        swap_kernel,
        out_shape=jax.ShapeDtypeStruct((n, per, 128), jnp.float32),
        in_specs=[vmem],
        out_specs=vmem,
        scratch_shapes=[
            pltpu.VMEM((n, per, 128), jnp.float32),
            pltpu.SemaphoreType.DMA,
            pltpu.SemaphoreType.DMA,
        ],
        compiler_params=pltpu.CompilerParams(collective_id=1, has_side_effects=True),
    )(tops)


def merge_kernel(inbox, shard_out, best_out):
    n, per = inbox.shape[:2]
    keep = shard_out.shape[2]
    lists = [inbox[:, q, :] for q in range(per)]
    for q in range(per):
        shard_out[q] = lists[q][:, :keep]
    column = jnp.concatenate(lists, axis=0)
    across = column.T
    width = per * n
    row = across[0:16, :]
    lane = lax.broadcasted_iota(jnp.int32, (16, width), 1)
    shard = lax.rem(lane, n)
    place = lax.broadcasted_iota(jnp.int32, (16, width), 0)

    def count(r, rank):
        near = pltpu.roll(row, r, 1)
        far = pltpu.roll(row, r + width - n, 1)
        wrapped = shard < r
        other = jnp.where(wrapped, far, near)
        for k in range(keep):
            rival = other[k : k + 1, :]
            ahead = (rival > row) | ((rival == row) & ~wrapped)
            rank = rank + ahead.astype(jnp.int32)
        return rank

    rank = lax.fori_loop(1, n, count, place)
    ranks = jnp.concatenate([rank, jnp.zeros((width - 16, width), jnp.int32)], axis=0).T
    target = lax.broadcasted_iota(jnp.int32, (width, 128), 1)
    found = jnp.zeros((width, 128), jnp.float32)
    for k in range(keep):
        found = found + jnp.where(ranks[:, k : k + 1] == target, column[:, k : k + 1], 0.0)
    for q in range(per):
        best = jnp.sum(found[q * n : (q + 1) * n, :], axis=0, keepdims=True)
        best_out[q : q + 1, :] = best[:, :TOPK]


def merge(inbox, keep):
    n, per, _ = inbox.shape
    vmem = pl.BlockSpec(memory_space=pltpu.VMEM)
    return pl.pallas_call(
        merge_kernel,
        out_shape=(
            jax.ShapeDtypeStruct((per, n, keep), jnp.float32),
            jax.ShapeDtypeStruct((per, TOPK), jnp.float32),
        ),
        in_specs=[vmem],
        out_specs=(vmem, vmem),
    )(inbox)


def local(
    queries,
    centroids,
    shard_table,
    token_refs,
    packed_residual_buckets,
    passage_lengths,
    bucket_values,
    candidates,
    live_counts,
):
    n, nz = lax.axis_size("cent"), lax.axis_size("qry")
    per, tokens, width = queries.shape[1:]
    z = lax.axis_index("qry")
    by_owner = shard_table.reshape(n, nz, -1)
    wanted = jnp.concatenate(
        [lax.dynamic_slice_in_dim(by_owner, quarter, 1, 1) for quarter in (z, lax.rem(z + 2, nz))], axis=1
    )
    table, resid, qcols, order = fetch(
        centroids, wanted, queries.reshape(per * tokens, width), passage_lengths[None, :], packed_residual_buckets,
        bucket_values,
    )
    tops = score(table.reshape(-1, width), token_refs, order, resid, qcols, candidates[0, 0], live_counts[0, 0])
    shard_tops, best_scores = merge(swap(tops, per), candidates.shape[3] // 4)
    return (shard_tops[None], best_scores[None])


def solution(mesh):
    return jax.shard_map(
        local,
        mesh=mesh,
        in_specs=(
            P("qry", "cent", None, None),
            P("cent", None),
            P("cent", None),
            P("cent", None),
            P("cent", None, None),
            P("cent"),
            P(),
            P("qry", "cent", None, None),
            P("qry", "cent", None),
        ),
        out_specs=(P("qry", "cent", None, None), P("qry", "cent", None)),
        check_vma=False,
    )
```

time: 526 us -> 114 us (0.22)
  local copies, waits for them, and re-layouts: 135 us -> 2.49 us
  other arithmetic: 132 us -> 0.63 us
  matrix products: 110 us -> 0 us
  Pallas kernels: 0 us -> 110 us
  waiting for transfers between devices: 52 us -> 0 us
  blocking collectives: 41 us -> 0 us
  loops' own time: 31.8 us -> 0 us
  between operations: 14.7 us -> 0.67 us
    gather x3 -> x0, local copies, waits for them, and re-layouts: 123 us -> none  [the longest x2 64 us: decode_shard(): jnp.take(tablevec, token_refs, axis=0)]
    reduce_sum x18 -> x0, other arithmetic: 114 us -> none  [the longest x1 109 us: decode_shard(): jnp.sum(summed * summed, axis=1, keepdims=True) + EPS]
    pallas_call x0 -> x4, Pallas kernels: none -> 110 us  [the longest x1 57.6 us: fetch(): pl.pallas_call(fetch_kernel, out_shape=(jax.ShapeDtypeStruct((n, nz, rows...]
    dot_general x16 -> x0, matrix products: 110 us -> none  [query_block_scores(): jnp.einsum('qtd,pdj->qtpj', query_tile_rows, embeds, preferred_element_ty...]
    all_to_all x1 -> x0, waiting for transfers between devices: 51.4 us -> none  [local(): lax.all_to_all(fetched, 'cent', split_axis=0, concat_axis=0, tiled=True)]
    another operation x1 -> x0, loops' own time: 31.8 us -> none  [local(): lax.map(query_block_scores, block_starts).reshape(qcount, passage_count)]
    all_gather x1 -> x0, blocking collectives: 25 us -> none  [local(): all_tops = lax.all_gather(local_tops[None], 'cent', axis=0, tiled=True)]
    all_to_all x1 -> x0, blocking collectives: 16 us -> none  [local(): lax.all_to_all(wanted, 'cent', split_axis=0, concat_axis=0, tiled=True)]
  transfers between devices with their start and end apart: 2 -> 0, of which waited for: 1 -> 0; matrix products, arithmetic and copies ran while one was open for 34% -> 0% of each run, Pallas kernels for 0% -> 0%
where the time goes in v2:
time: 114 us
  Pallas kernels  110 us (96%)
  local copies, waits for them, and re-layouts  2.49 us (2%)
    pallas_call x1, Pallas kernels, fetch(): pl.pallas_call(fetch_kernel, out_shape=(jax.ShapeDtypeStruct((n, nz, rows...  57.6 us
    pallas_call x1, Pallas kernels, score(): pl.pallas_call(score_kernel, out_shape=jax.ShapeDtypeStruct((queries, 128...  34.4 us
    pallas_call x1, Pallas kernels, swap(): pl.pallas_call(swap_kernel, out_shape=jax.ShapeDtypeStruct((n, per, 128),...  13 us
    pallas_call x1, Pallas kernels, merge(): pl.pallas_call(merge_kernel, out_shape=(jax.ShapeDtypeStruct((per, n, kee...  5.18 us

profile of v2, /device:TPU:1, one launch (start us, length us, event | category | flops | bytes accessed | tf_op | source)
XLA Modules:
  0.0 114.0 jit_solution(1562866973904608308)
XLA Ops:
  0.6 1.0 constant_dynamic-slice_fusion.1
  1.6 0.6 pad_add_fusion.wanted
  2.2 57.6 %shard_map.104 = (bf16[32,4,128,128]{3,2,1,0:T(8,128)(2,1)}, f32[16,1024,128]{2,1,0:T(8,128)}, bf16[128,4096]{1,0:T(8,128)(2,1)}, s32[8,128]{1,0:T(8,128)}) custom-call(bf16[32768,128]{1,0:T(8,128)(2,1)} %cent_hbm.1, s32[32,2,128]{2,1,0:T(2,128)} %pad_add_fusion.wanted, bf16[128,128]{1,0:T(8,128)(2,1)} %bitcast.14, s32[1,128]{1,0:T(1,128)} %bitcast.17, ...), custom_call_target="tpu_custom_call" | custom-call | tf_op jit(solution)/shard_map/pallas_call | solution.py:233
  59.8 34.4 %shard_map.105.tops = f32[128,128]{1,0:T(8,128)} custom-call(s32[16384]{0:T(1024)} %bitcast.12, s32[8,128]{1,0:T(8,128)} %get-tuple-element.8.order.order_ref, s32[8,128]{1,0:T(8,128)} %get-tuple-element.8.order.order_ref, bf16[16384,128]{1,0:T(8,128)(2,1)} %bitcast.11, f32[16,1024,128]{2,1,0:T(8,128)} %get-tuple-element.10.resid_hbm, ...), custom_call_target="tpu_custom_call" | custom-call | tf_op jit(solution)/shard_map/pallas_call | solution.py:421
  94.2 13.0 %shard_map.106.inbox = f32[32,4,128]{2,1,0:T(4,128)} custom-call(f32[128,128]{1,0:T(8,128)} %shard_map.105.tops), custom_call_target="tpu_custom_call" | custom-call | tf_op jit(solution)/shard_map/pallas_call | solution.py:477
  107.3 5.2 %shard_map.107 = (f32[4,32,12]{2,1,0:T(8,128)}, f32[4,100]{1,0:T(4,128)}) custom-call(f32[32,4,128]{2,1,0:T(4,128)} %shard_map.106.inbox), custom_call_target="tpu_custom_call" | custom-call | tf_op jit(solution)/shard_map/pallas_call | solution.py:530
  112.4 1.5 %copy.11 = f32[1,4,32,12]{2,1,3,0:T(4,128)} copy(f32[1,4,32,12]{3,2,1,0:T(8,128)} %bitcast.13) | data formatting | bytes 12288

commit v3 on v2

--- a/solution.py
+++ b/solution.py
@@ -1,3 +1,5 @@
+import functools
+
 import jax
 import jax.numpy as jnp
 from jax import lax
@@ -13,19 +15,49 @@
 CHUNK = 512
 UNIT = 4
 MESH = pl.DeviceIdType.MESH
+CENT_AXES = (4, 4, 2)
+HOPS = (
+    (1, 0), (0, 1), (3, 0), (0, 3), (1, 1), (3, 3), (1, 3), (3, 1),
+    (2, 0), (0, 2), (2, 1), (1, 2), (2, 3), (3, 2), (2, 2),
+)
+PART = 112
+
+
+def place_of(me):
+    wide, deep, cores = CENT_AXES
+    return lax.div(me, deep * cores), lax.rem(lax.div(me, cores), deep), lax.rem(me, cores)
+
+
+def peer_of(me, i, sign):
+    wide, deep, cores = CENT_AXES
+    x, y, core = place_of(me)
+    many = len(HOPS)
+    j, other = lax.rem(i - 1, many), lax.div(i - 1, many)
+    code = 0
+    for t, (dx, dy) in enumerate(HOPS):
+        code = code + jnp.where(j == t, dx * deep + dy, 0)
+    last = i == cores * many + 1
+    code = jnp.where(last, 0, code)
+    other = jnp.where(last, 1, other)
+    dx, dy = lax.div(code, deep), lax.rem(code, deep)
+    if sign < 0:
+        dx, dy = wide - dx, deep - dy
+    x, y, core = lax.rem(x + dx, wide), lax.rem(y + dy, deep), lax.rem(core + other, cores)
+    return (x * deep + y) * cores + core
 
 
 def fetch_kernel(
-    cent_hbm, wanted, own, lengths, packed, buckets, tab, resid_hbm, qcols, order,
-    stage, cent, asked, asked_s, sbuf, qall, qwide, spread, resid, order_s,
-    stage_sem, asked_sem, order_sem, own_sem, resid_sem, off_send, off_recv,
-    q_send, q_recv, pair_send, pair_recv, blk_send, blk_recv, half_recv, z_send, left_recv, right_recv, far_recv,
+    tokens, cent_hbm, wanted, own, lengths, packed_hbm, buckets, tab, resid_hbm, qcols, order,
+    packed, stage, cent, mid, asked, asked_s, sbuf, qall, qwide, spread, resid, order_s,
+    packed_sem, stage_sem, asked_sem, order_sem, own_sem, resid_sem, off_send, off_recv, row_send, row_recv,
+    q_send, q_recv, q_row_send, q_row_recv, pair_send, pair_recv, blk_send, blk_recv, half_recv, z_send, left_recv, right_recv, far_recv,
 ):
     me, z = lax.axis_index("cent"), lax.axis_index("qry")
     n, nz = lax.axis_size("cent"), lax.axis_size("qry")
-    core = lax.rem(me, 2)
-    chip = lax.div(me, 2)
-    chips = n // 2
+    wide, deep, cores = CENT_AXES
+    line_size = deep * cores
+    mx, my, core = place_of(me)
+    mr = lax.rem(me, line_size)
     right, far, left = lax.rem(z + 1, nz), lax.rem(z + 2, nz), lax.rem(z + 3, nz)
     rows = tab.shape[2]
     part = sbuf.shape[1] - rows
@@ -43,12 +75,20 @@
     for load in loads:
         load.start()
 
+    load_packed = pltpu.make_async_copy(packed_hbm, packed, packed_sem)
+    load_packed.start()
+
+    def in_row(i):
+        return mx * line_size + lax.rem(mr + i, line_size)
+
+    def in_column(i):
+        return lax.rem(mx + i, wide) * line_size + mr
+
     barrier = pltpu.get_barrier_semaphore()
-
-    @pl.loop(1, n)
-    def _(i):
-        pl.semaphore_signal(barrier, inc=1, device_id=(lax.rem(me + i, n), z), device_id_type=MESH)
-
+    for i in range(1, line_size):
+        pl.semaphore_signal(barrier, inc=1, device_id=(in_row(i), z), device_id_type=MESH)
+    for i in range(1, wide):
+        pl.semaphore_signal(barrier, inc=1, device_id=(in_column(i), z), device_id_type=MESH)
     for side in (left, right, far):
         pl.semaphore_signal(barrier, inc=1, device_id=(me, side), device_id_type=MESH)
 
@@ -77,66 +117,75 @@
                 cent[at, :] = stage[at, :].astype(jnp.float32)
 
     widen(0, pieces // 2)
-    pl.semaphore_wait(barrier, n + 2)
-
-    @pl.loop(1, n)
-    def _(i):
-        peer = lax.rem(me + i, n)
-        pltpu.make_async_remote_copy(
-            src_ref=wanted.at[peer], dst_ref=asked.at[me], send_sem=off_send, recv_sem=off_recv,
-            device_id=(peer, z), device_id_type=MESH,
-        ).start()
-
-    asked[me] = wanted[me]
-    qall[chip, core] = own[...]
+    pl.semaphore_wait(barrier, line_size + wide - 2 + 3)
+
+    def remote(src, dst, send, recv, peer):
+        return pltpu.make_async_remote_copy(
+            src_ref=src, dst_ref=dst, send_sem=send, recv_sem=recv, device_id=(peer, z), device_id_type=MESH
+        )
+
+    for i in range(1, line_size):
+        remote(wanted.at[lax.rem(mr + i, line_size)], mid.at[mr], off_send, off_recv, in_row(i)).start()
+    for i in range(1, wide):
+        remote(own, qall.at[mx, my, core], q_send, q_recv, in_column(i)).start()
+    mid[mr] = wanted[mr]
+    qall[mx, my, core] = own[...]
     widen(pieces // 2, pieces)
     to_order.wait()
-
-    offsets = pltpu.make_async_remote_copy(
-        src_ref=wanted.at[pl.ds(0, n - 1)], dst_ref=asked.at[pl.ds(0, n - 1)],
-        send_sem=off_send, recv_sem=off_recv, device_id=(lax.rem(me + 1, n), z), device_id_type=MESH,
+    load_packed.wait()
+    first = remote(
+        wanted.at[pl.ds(0, line_size - 1)], mid.at[pl.ds(0, line_size - 1)], off_send, off_recv, in_row(1)
     )
-    offsets.wait_recv()
+    first.wait_recv()
+    for i in range(1, wide):
+        remote(mid.at[:, lax.rem(mx + i, wide)], asked.at[mx], row_send, row_recv, in_column(i)).start()
+    asked[mx] = mid[:, mx]
+    remote(qall.at[pl.ds(0, wide - 1), 0, 0], qall.at[pl.ds(0, wide - 1), 0, 0], q_send, q_recv, in_column(1)).wait_recv()
+    for i in range(1, deep):
+        peer = (mx * deep + lax.rem(my + i, deep)) * cores + core
+        remote(qall.at[:, my, core], qall.at[:, my, core], q_row_send, q_row_recv, peer).start()
+    second = remote(
+        asked.at[pl.ds(0, wide - 1)], asked.at[pl.ds(0, wide - 1)], row_send, row_recv, in_column(1)
+    )
+    second.wait_recv()
     to_scalar = pltpu.make_async_copy(asked, asked_s, asked_sem)
     to_scalar.start()
     to_scalar.wait()
 
     sub = lax.broadcasted_iota(jnp.int32, (16, 128), 0)
 
-    def pull(i, line, start, count):
-        peer = lax.rem(me + i, n)
+    def pull(i, peer, line, start, count):
+        px, pr = lax.div(peer, line_size), lax.rem(peer, line_size)
         for r in range(0, count, 16):
-            tile = jnp.broadcast_to(cent[pl.ds(asked_s[peer, line, r], 1), :], (16, 128))
+            tile = jnp.broadcast_to(cent[pl.ds(asked_s[px, pr, line, r], 1), :], (16, 128))
             for k in range(1, 16):
-                value = jnp.broadcast_to(cent[pl.ds(asked_s[peer, line, r + k], 1), :], (16, 128))
+                value = jnp.broadcast_to(cent[pl.ds(asked_s[px, pr, line, r + k], 1), :], (16, 128))
                 tile = jnp.where(sub == k, value, tile)
             sbuf[i, start + r : start + r + 16, :] = tile.astype(jnp.bfloat16)
 
-    def block_copy(i):
-        return pltpu.make_async_remote_copy(
-            src_ref=sbuf.at[i, pl.ds(0, rows)], dst_ref=tab.at[me, z], send_sem=blk_send, recv_sem=blk_recv.at[i],
-            device_id=(lax.rem(me + i, n), z), device_id_type=MESH,
-        )
-
-    pull(0, 0, 0, rows)
+    def block_copy(i, peer):
+        return remote(sbuf.at[i, pl.ds(0, rows)], tab.at[me, z], blk_send, blk_recv.at[i], peer)
+
+    pull(0, me, 0, 0, rows)
     keep_own = pltpu.make_async_copy(sbuf.at[0, pl.ds(0, rows)], tab.at[me, z], own_sem.at[0])
     keep_own.start()
 
     @pl.loop(1, n)
     def _(i):
-        pull(i, 0, 0, rows)
-        block_copy(i).start()
+        peer = peer_of(me, i, 1)
+        pull(i, peer, 0, 0, rows)
+        block_copy(i, peer).start()
 
     def along(ref, side, recv):
         return pltpu.make_async_remote_copy(
             src_ref=ref, dst_ref=ref, send_sem=z_send, recv_sem=recv, device_id=(me, side), device_id_type=MESH,
         )
 
-    def forward(k):
-        owner = lax.rem(me + n - k, n)
+    def forward(owner):
         along(tab.at[owner, z], right, left_recv).start()
         along(tab.at[owner, z], left, right_recv).start()
-        along(tab.at[owner, z, pl.ds(part, rows - part)], far, far_recv).start()
+        if part < rows:
+            along(tab.at[owner, z, pl.ds(part, rows - part)], far, far_recv).start()
 
     def decode(i):
         words = packed[order_s[0, i]]
@@ -146,113 +195,122 @@
         value = jnp.where(digits < 2, low, high)
         resid[lax.div(i, 8), pl.ds(lax.rem(i, 8), ptok, stride=8), :] = value.T
 
-    def extras(k):
+    def extras(k, peer):
         for j in range(passages // n):
             decode(k * (passages // n) + j)
-        pull(k, 1, rows, part)
+        pull(k, peer, 1, rows, part)
 
     def save(g):
         return pltpu.make_async_copy(resid.at[g], resid_hbm.at[g], resid_sem)
-
-    keep_own.wait()
-    forward(0)
-    extras(0)
-    keep_half = pltpu.make_async_copy(sbuf.at[0, pl.ds(rows, part)], tab.at[me, far, pl.ds(0, part)], own_sem.at[1])
-    keep_half.start()
-
-    @pl.loop(1, n)
-    def _(k):
-        block_copy(k).wait_recv()
-        forward(k)
-        extras(k)
-        pltpu.make_async_remote_copy(
-            src_ref=sbuf.at[k, pl.ds(rows, part)], dst_ref=tab.at[me, far, pl.ds(0, part)],
-            send_sem=blk_send, recv_sem=half_recv,
-            device_id=(lax.rem(me + k, n), z), device_id_type=MESH,
-        ).start()
-
-        @pl.when(lax.rem(k, 2) == 0)
-        def _():
-            pltpu.make_async_remote_copy(
-                src_ref=own, dst_ref=qall.at[chip, core], send_sem=q_send, recv_sem=q_recv,
-                device_id=(lax.rem(me + k, n), z), device_id_type=MESH,
-            ).start()
-
-        @pl.when(lax.rem(k, 2) == 1)
-        def _():
-            save(lax.div(k, 2)).start()
 
     def bulk(ref, send, recv):
         return pltpu.make_async_remote_copy(
             src_ref=ref, dst_ref=ref, send_sem=send, recv_sem=recv, device_id=(me, right), device_id_type=MESH,
         )
 
-    bulk(qall.at[pl.ds(0, chips - 1), 0], q_send, q_recv).wait_recv()
-    pair = pltpu.make_async_remote_copy(
-        src_ref=qall.at[pl.ds(0, chips), core], dst_ref=qall.at[pl.ds(0, chips), core],
-        send_sem=pair_send, recv_sem=pair_recv,
-        device_id=(me + 1 - 2 * core, z), device_id_type=MESH,
-    )
+    keep_own.wait()
+    forward(me)
+    extras(0, me)
+    keep_half = pltpu.make_async_copy(sbuf.at[0, pl.ds(rows, part)], tab.at[me, far, pl.ds(0, part)], own_sem.at[1])
+    keep_half.start()
+
+    def relay(k):
+        peer = peer_of(me, k, 1)
+        block_copy(k, peer).wait_recv()
+        forward(peer_of(me, k, -1))
+        extras(k, peer)
+        remote(
+            sbuf.at[k, pl.ds(rows, part)], tab.at[me, far, pl.ds(0, part)], blk_send, half_recv, peer
+        ).start()
+
+        @pl.when(lax.rem(k, 2) == 1)
+        def _():
+            save(lax.div(k, 2)).start()
+
+    per = own.shape[0]
+    queries = qcols.shape[1] // tokens
+
+    @pl.loop(1, n // 2)
+    def _(k):
+        relay(k)
+
+    bulk(qall.at[pl.ds(0, wide), pl.ds(0, deep - 1), 0], q_row_send, q_row_recv).wait_recv()
+    pair = remote(qall.at[:, :, core], qall.at[:, :, core], pair_send, pair_recv, me + 1 - 2 * core)
     pair.start()
+
+    @pl.loop(n // 2, n // 4 * 3)
+    def _(k):
+        relay(k)
+
     pair.wait()
 
-    tokens = own.shape[0] * n // passages
-    per = own.shape[0]
-
-    @pl.loop(0, chips)
+    @pl.loop(0, wide)
     def _(i):
-        for c in range(2):
-            qwide[pl.ds(pl.multiple_of((i * 2 + c) * per, per), per), :] = qall[i, c].astype(jnp.float32)
+        for y in range(deep):
+            for c in range(cores):
+                at = i * (line_size * per) + (y * cores + c) * per
+                qwide[pl.ds(pl.multiple_of(at, per), per), :] = qall[i, y, c].astype(jnp.float32)
 
     for t in range(tokens):
-        tile = qwide[pl.ds(t, passages, stride=tokens), :]
-        qcols[:, t * passages : (t + 1) * passages] = tile.T.astype(jnp.bfloat16)
+        tile = qwide[pl.ds(t, queries, stride=tokens), :]
+        qcols[:, t * queries : (t + 1) * queries] = tile.T.astype(jnp.bfloat16)
+
+    @pl.loop(n // 4 * 3, n)
+    def _(k):
+        relay(k)
 
     bulk(tab.at[pl.ds(0, n // nz)], z_send, left_recv).wait_recv()
     bulk(tab.at[pl.ds(0, n // nz)], z_send, right_recv).wait_recv()
-    bulk(tab.at[pl.ds(0, n), 0, pl.ds(part, rows - part)], z_send, far_recv).wait_recv()
+    if part < rows:
+        bulk(tab.at[pl.ds(0, n), 0, pl.ds(part, rows - part)], z_send, far_recv).wait_recv()
     bulk(sbuf.at[pl.ds(0, n - 1), pl.ds(rows, part)], z_send, half_recv).wait_recv()
     keep_half.wait()
     pltpu.make_async_copy(resid, resid_hbm, resid_sem).wait()
-    offsets.wait_send()
-    bulk(qall.at[pl.ds(0, chips - 1), 0], q_send, q_recv).wait_send()
+    first.wait_send()
+    second.wait_send()
+    bulk(qall.at[pl.ds(0, wide - 1), 0, 0], q_send, q_recv).wait_send()
+    bulk(qall.at[pl.ds(0, wide), pl.ds(0, deep - 1), 0], q_row_send, q_row_recv).wait_send()
     bulk(sbuf.at[pl.ds(0, n - 1)], blk_send, q_recv).wait_send()
     bulk(tab.at[pl.ds(0, 2 * n // nz)], z_send, q_recv).wait_send()
-    bulk(tab.at[pl.ds(0, n), 0, pl.ds(part, rows - part)], z_send, q_recv).wait_send()
-
-
-def fetch(centroids, wanted, own, lengths, packed, buckets):
+    if part < rows:
+        bulk(tab.at[pl.ds(0, n), 0, pl.ds(part, rows - part)], z_send, q_recv).wait_send()
+
+
+def fetch(centroids, wanted, own, lengths, packed, buckets, tokens):
     n, nz = lax.axis_size("cent"), lax.axis_size("qry")
-    rows = wanted.shape[2]
-    part = rows // 2
+    wide, deep, cores = CENT_AXES
+    rows = wanted.shape[3]
+    part = PART
     passages, _, ptok = packed.shape
     vmem = pl.BlockSpec(memory_space=pltpu.VMEM)
     hbm = pl.BlockSpec(memory_space=pl.ANY)
     dma = pltpu.SemaphoreType.DMA
     groups = passages // 8
     return pl.pallas_call(
-        fetch_kernel,
+        functools.partial(fetch_kernel, tokens),
         out_shape=(
             jax.ShapeDtypeStruct((n, nz, rows, 128), jnp.bfloat16),
             jax.ShapeDtypeStruct((groups, 8 * ptok, 128), jnp.float32),
             jax.ShapeDtypeStruct((128, n * own.shape[0]), jnp.bfloat16),
             jax.ShapeDtypeStruct((8, passages), jnp.int32),
         ),
-        in_specs=[hbm, vmem, vmem, vmem, vmem, vmem],
+        in_specs=[hbm, vmem, vmem, vmem, hbm, vmem],
         out_specs=(hbm, hbm, vmem, vmem),
         scratch_shapes=[
+            pltpu.VMEM(packed.shape, jnp.int32),
             pltpu.VMEM(centroids.shape, jnp.bfloat16),
             pltpu.VMEM(centroids.shape, jnp.float32),
-            pltpu.VMEM((n, 2, rows), jnp.int32),
-            pltpu.SMEM((n, 2, rows), jnp.int32),
+            pltpu.VMEM((deep * cores, wide, 2, rows), jnp.int32),
+            pltpu.VMEM((wide, deep * cores, 2, rows), jnp.int32),
+            pltpu.SMEM((wide, deep * cores, 2, rows), jnp.int32),
             pltpu.VMEM((n, rows + part, 128), jnp.bfloat16),
-            pltpu.VMEM((n // 2, 2) + own.shape, jnp.bfloat16),
+            pltpu.VMEM(CENT_AXES + own.shape, jnp.bfloat16),
             pltpu.VMEM((n * own.shape[0], 128), jnp.float32),
             pltpu.VMEM((4, 128, ptok), jnp.float32),
             pltpu.VMEM((groups, 8 * ptok, 128), jnp.float32),
             pltpu.SMEM((8, passages), jnp.int32),
-            dma((8,)), dma, dma, dma((2,)), dma, dma, dma,
-            dma, dma, dma, dma, dma, dma((n,)), dma, dma, dma, dma, dma,
+            dma, dma((8,)), dma, dma, dma((2,)), dma, dma, dma, dma, dma,
+            dma, dma, dma, dma, dma, dma, dma, dma((n,)), dma, dma, dma, dma, dma,
         ],
         compiler_params=pltpu.CompilerParams(
             collective_id=0, has_side_effects=True, vmem_limit_bytes=58 * 2**20
@@ -442,67 +500,83 @@
     )(refs.reshape(-1), order, order, table, resid, qcols, cand.T, live[None, :])
 
 
-def swap_kernel(tops, inbox, outbox, send_sem, recv_sem):
+def swap_kernel(tops, inbox, outbox, mid, row_send, row_recv, send, recv):
     me, z = lax.axis_index("cent"), lax.axis_index("qry")
-    n = lax.axis_size("cent")
-    per = outbox.shape[1]
+    wide, deep, cores = CENT_AXES
+    line_size = deep * cores
+    mx, mr = lax.div(me, line_size), lax.rem(me, line_size)
+    per = outbox.shape[2]
+
+    def in_row(i):
+        return mx * line_size + lax.rem(mr + i, line_size)
+
+    def in_column(i):
+        return lax.rem(mx + i, wide) * line_size + mr
+
     barrier = pltpu.get_barrier_semaphore()
-
-    @pl.loop(1, n)
-    def _(i):
-        pl.semaphore_signal(barrier, inc=1, device_id=(lax.rem(me + i, n), z), device_id_type=MESH)
-
-    for i in range(tops.shape[0] // per):
-        outbox[i] = tops[i * per : (i + 1) * per, :]
-    inbox[me] = outbox[me]
-    pl.semaphore_wait(barrier, n - 1)
-
-    @pl.loop(1, n)
-    def _(i):
-        peer = lax.rem(me + i, n)
-        pltpu.make_async_remote_copy(
-            src_ref=outbox.at[peer], dst_ref=inbox.at[me], send_sem=send_sem, recv_sem=recv_sem,
-            device_id=(peer, z), device_id_type=MESH,
-        ).start()
-
-    pltpu.make_async_remote_copy(
-        src_ref=outbox.at[pl.ds(0, n - 1)], dst_ref=inbox.at[pl.ds(0, n - 1)],
-        send_sem=send_sem, recv_sem=recv_sem, device_id=(lax.rem(me + 1, n), z), device_id_type=MESH,
-    ).wait()
+    for i in range(1, line_size):
+        pl.semaphore_signal(barrier, inc=1, device_id=(in_row(i), z), device_id_type=MESH)
+    for i in range(1, wide):
+        pl.semaphore_signal(barrier, inc=1, device_id=(in_column(i), z), device_id_type=MESH)
+    for x in range(wide):
+        for r in range(line_size):
+            at = (x * line_size + r) * per
+            outbox[r, x] = tops[at : at + per, :]
+    mid[mr] = outbox[mr]
+    pl.semaphore_wait(barrier, line_size + wide - 2)
+
+    def remote(src, dst, send_sem, recv_sem, peer):
+        return pltpu.make_async_remote_copy(
+            src_ref=src, dst_ref=dst, send_sem=send_sem, recv_sem=recv_sem, device_id=(peer, z), device_id_type=MESH
+        )
+
+    for i in range(1, line_size):
+        remote(outbox.at[lax.rem(mr + i, line_size)], mid.at[mr], row_send, row_recv, in_row(i)).start()
+    most = pl.ds(0, line_size - 1)
+    remote(outbox.at[most], mid.at[most], row_send, row_recv, in_row(1)).wait()
+    for i in range(1, wide):
+        remote(mid.at[:, lax.rem(mx + i, wide)], inbox.at[mx], send, recv, in_column(i)).start()
+    inbox[mx] = mid[:, mx]
+    most = pl.ds(0, wide - 1)
+    remote(inbox.at[most], inbox.at[most], send, recv, in_column(1)).wait()
 
 
 def swap(tops, per):
     n = lax.axis_size("cent")
+    wide, deep, cores = CENT_AXES
     vmem = pl.BlockSpec(memory_space=pltpu.VMEM)
-    return pl.pallas_call(
+    dma = pltpu.SemaphoreType.DMA
+    inbox = pl.pallas_call(
         swap_kernel,
-        out_shape=jax.ShapeDtypeStruct((n, per, 128), jnp.float32),
+        out_shape=jax.ShapeDtypeStruct((wide, deep * cores, per, 128), jnp.float32),
         in_specs=[vmem],
         out_specs=vmem,
         scratch_shapes=[
-            pltpu.VMEM((n, per, 128), jnp.float32),
-            pltpu.SemaphoreType.DMA,
-            pltpu.SemaphoreType.DMA,
+            pltpu.VMEM((deep * cores, wide, per, 128), jnp.float32),
+            pltpu.VMEM((deep * cores, wide, per, 128), jnp.float32),
+            dma, dma, dma, dma,
         ],
         compiler_params=pltpu.CompilerParams(collective_id=1, has_side_effects=True),
     )(tops)
+    return inbox.reshape(n, per, 128)
 
 
 def merge_kernel(inbox, shard_out, best_out):
     n, per = inbox.shape[:2]
-    keep = shard_out.shape[2]
+    keep = shard_out.shape[0]
     lists = [inbox[:, q, :] for q in range(per)]
-    for q in range(per):
-        shard_out[q] = lists[q][:, :keep]
     column = jnp.concatenate(lists, axis=0)
     across = column.T
     width = per * n
     row = across[0:16, :]
+    for q in range(per):
+        shard_out[:, q, :] = row[:keep, q * n : (q + 1) * n]
     lane = lax.broadcasted_iota(jnp.int32, (16, width), 1)
     shard = lax.rem(lane, n)
     place = lax.broadcasted_iota(jnp.int32, (16, width), 0)
 
-    def count(r, rank):
+    rank = place
+    for r in range(1, n):
         near = pltpu.roll(row, r, 1)
         far = pltpu.roll(row, r + width - n, 1)
         wrapped = shard < r
@@ -511,9 +585,6 @@
             rival = other[k : k + 1, :]
             ahead = (rival > row) | ((rival == row) & ~wrapped)
             rank = rank + ahead.astype(jnp.int32)
-        return rank
-
-    rank = lax.fori_loop(1, n, count, place)
     ranks = jnp.concatenate([rank, jnp.zeros((width - 16, width), jnp.int32)], axis=0).T
     target = lax.broadcasted_iota(jnp.int32, (width, 128), 1)
     found = jnp.zeros((width, 128), jnp.float32)
@@ -530,7 +601,7 @@
     return pl.pallas_call(
         merge_kernel,
         out_shape=(
-            jax.ShapeDtypeStruct((per, n, keep), jnp.float32),
+            jax.ShapeDtypeStruct((keep, per, n), jnp.float32),
             jax.ShapeDtypeStruct((per, TOPK), jnp.float32),
         ),
         in_specs=[vmem],
@@ -556,13 +627,14 @@
     wanted = jnp.concatenate(
         [lax.dynamic_slice_in_dim(by_owner, quarter, 1, 1) for quarter in (z, lax.rem(z + 2, nz))], axis=1
     )
+    wanted = jnp.swapaxes(wanted.reshape((CENT_AXES[0], n // CENT_AXES[0]) + wanted.shape[1:]), 0, 1)
     table, resid, qcols, order = fetch(
         centroids, wanted, queries.reshape(per * tokens, width), passage_lengths[None, :], packed_residual_buckets,
-        bucket_values,
+        bucket_values, tokens,
     )
     tops = score(table.reshape(-1, width), token_refs, order, resid, qcols, candidates[0, 0], live_counts[0, 0])
     shard_tops, best_scores = merge(swap(tops, per), candidates.shape[3] // 4)
-    return (shard_tops[None], best_scores[None])
+    return (jnp.transpose(shard_tops, (1, 2, 0))[None], best_scores[None])
 
 
 def solution(mesh):

time: 114 us -> 106 us (0.930)
  Pallas kernels: 110 us -> 103 us
    pallas_call x3, Pallas kernels: 75.7 us -> 68.7 us  [the longest x1 51.1 us: fetch(): pl.pallas_call(functools.partial(fetch_kernel, tokens), out_shape=(jax.Sh...]
    unnamed x1 -> x0, local copies, waits for them, and re-layouts: 1.54 us -> none
where the time goes in v3:
time: 106 us; the launch traced here: 105 us
  Pallas kernels  103 us (97%)
  local copies, waits for them, and re-layouts  1.57 us (1%)
    pallas_call x1, Pallas kernels, fetch(): pl.pallas_call(functools.partial(fetch_kernel, tokens), out_shape=(jax.Sh...  51.1 us
    pallas_call x1, Pallas kernels, score(): pl.pallas_call(score_kernel, out_shape=jax.ShapeDtypeStruct((queries, 128...  34.4 us
    pallas_call x1, Pallas kernels, swap(): pl.pallas_call(swap_kernel, out_shape=jax.ShapeDtypeStruct((wide, deep *...  14.8 us
    pallas_call x1, Pallas kernels, merge(): pl.pallas_call(merge_kernel, out_shape=(jax.ShapeDtypeStruct((keep, per,...  2.83 us

profile of v3, /device:TPU:1, one launch (start us, length us, event | category | flops | bytes accessed | tf_op | source)
XLA Modules:
  0.0 105.4 jit_solution(11853456516657675621)
XLA Ops:
  0.6 1.0 constant_dynamic-slice_fusion.1
  1.6 0.6 copy.17
  2.2 51.1 %shard_map.104 = (bf16[32,4,128,128]{3,2,1,0:T(8,128)(2,1)}, f32[16,1024,128]{2,1,0:T(8,128)}, bf16[128,4096]{1,0:T(8,128)(2,1)}, s32[8,128]{1,0:T(8,128)}) custom-call(bf16[32768,128]{1,0:T(8,128)(2,1)} %cent_hbm.1, s32[8,4,2,128]{3,2,1,0:T(2,128)} %bitcast.20, bf16[128,128]{1,0:T(8,128)(2,1)} %bitcast.23, s32[1,128]{1,0:T(1,128)} %bitcast.26, ...), custom_call_target="tpu_custom_call" | custom-call | tf_op jit(solution)/shard_map/pallas_call | solution.py:289
  53.3 34.4 %shard_map.105.tops = f32[128,128]{1,0:T(8,128)} custom-call(s32[16384]{0:T(1024)} %bitcast.22, s32[8,128]{1,0:T(8,128)} %get-tuple-element.8.order.order_ref, s32[8,128]{1,0:T(8,128)} %get-tuple-element.8.order.order_ref, bf16[16384,128]{1,0:T(8,128)(2,1)} %bitcast.18, f32[16,1024,128]{2,1,0:T(8,128)} %get-tuple-element.10.resid_hbm, ...), custom_call_target="tpu_custom_call" | custom-call | tf_op jit(solution)/shard_map/pallas_call | solution.py:479
  87.8 14.8 %shard_map.106 = f32[4,8,4,128]{3,2,1,0:T(4,128)} custom-call(f32[128,128]{1,0:T(8,128)} %shard_map.105.tops), custom_call_target="tpu_custom_call" | custom-call | tf_op jit(solution)/shard_map/pallas_call | solution.py:549
  102.6 2.8 %shard_map.107 = (f32[12,4,32]{2,1,0:T(4,128)}, f32[4,100]{1,0:T(4,128)}) custom-call(f32[32,4,128]{2,1,0:T(4,128)} %bitcast.19), custom_call_target="tpu_custom_call" | custom-call | tf_op jit(solution)/shard_map/pallas_call | solution.py:601
  (1 shorter events, 0.0 us)

commit v4 on v3

--- a/solution.py
+++ b/solution.py
@@ -1,5 +1,3 @@
-import functools
-
 import jax
 import jax.numpy as jnp
 from jax import lax
@@ -12,15 +10,15 @@
 EPS = 1e-6
 LOW = float("-inf")
 TB = 16
-CHUNK = 512
-UNIT = 4
+GROUP = 4
+TILES = 4
 MESH = pl.DeviceIdType.MESH
 CENT_AXES = (4, 4, 2)
 HOPS = (
     (1, 0), (0, 1), (3, 0), (0, 3), (1, 1), (3, 3), (1, 3), (3, 1),
     (2, 0), (0, 2), (2, 1), (1, 2), (2, 3), (3, 2), (2, 2),
 )
-PART = 112
+PART = 128
 
 
 def place_of(me):
@@ -47,10 +45,10 @@
 
 
 def fetch_kernel(
-    tokens, cent_hbm, wanted, own, lengths, packed_hbm, buckets, tab, resid_hbm, qcols, order,
-    packed, stage, cent, mid, asked, asked_s, sbuf, qall, qwide, spread, resid, order_s,
+    cent_hbm, wanted, own, lengths, packed_hbm, buckets, cand, live, tab, resid_hbm, qall, order, members, place,
+    packed, stage, cent, mid, asked, asked_s, sbuf, spread, resid, spots, order_s,
     packed_sem, stage_sem, asked_sem, order_sem, own_sem, resid_sem, off_send, off_recv, row_send, row_recv,
-    q_send, q_recv, q_row_send, q_row_recv, pair_send, pair_recv, blk_send, blk_recv, half_recv, z_send, left_recv, right_recv, far_recv,
+    q_send, q_recv, q_row_send, q_row_recv, pair_send, pair_recv, blk_send, blk_recv, half_recv, z_send, left_recv, right_recv,
 ):
     me, z = lax.axis_index("cent"), lax.axis_index("qry")
     n, nz = lax.axis_size("cent"), lax.axis_size("qry")
@@ -61,6 +59,7 @@
     right, far, left = lax.rem(z + 1, nz), lax.rem(z + 2, nz), lax.rem(z + 3, nz)
     rows = tab.shape[2]
     part = sbuf.shape[1] - rows
+    slots, queries = cand.shape
     pieces = stage_sem.shape[0]
     depth = stage.shape[0] // pieces
     passages = packed.shape[0]
@@ -89,7 +88,7 @@
         pl.semaphore_signal(barrier, inc=1, device_id=(in_row(i), z), device_id_type=MESH)
     for i in range(1, wide):
         pl.semaphore_signal(barrier, inc=1, device_id=(in_column(i), z), device_id_type=MESH)
-    for side in (left, right, far):
+    for side in (left, right):
         pl.semaphore_signal(barrier, inc=1, device_id=(me, side), device_id_type=MESH)
 
     across = jnp.broadcast_to(lengths[...], (passages, passages))
@@ -101,7 +100,42 @@
     hit = jnp.broadcast_to(rank, (passages, passages)).T == lane
     order[0:1, :] = jnp.sum(jnp.where(hit, line, 0), axis=0, keepdims=True)
     order[1:2, :] = jnp.sum(jnp.where(hit, down, 0), axis=0, keepdims=True)
-    order[2:8, :] = jnp.zeros((6, passages), jnp.int32)
+    lens = order[1:2, :]
+    owner_of = jnp.broadcast_to(order[0:1, :], (passages, queries)).T
+
+    def mark(slot, need):
+        hit = (owner_of == cand[pl.ds(slot, 1), :]) & (live[...] > slot)
+        return jnp.where(hit, 1.0, need)
+
+    need = lax.fori_loop(0, slots, mark, jnp.zeros((passages, queries), jnp.float32), unroll=4)
+    flags = need.astype(jnp.bfloat16)
+    before = (line < lane).astype(jnp.bfloat16)
+    spot = jnp.dot(flags, before, preferred_element_type=jnp.float32)
+    place[...] = jnp.where(need > 0, spot, 0.0).astype(jnp.int32)
+    spots[...] = jnp.where(need > 0, spot, -1.0)
+    across_lanes = (((1,), (1,)), ((), ()))
+    counts = lax.dot_general(
+        jnp.ones((8, queries), jnp.bfloat16), flags, across_lanes, preferred_element_type=jnp.float32
+    )[0:1]
+    order[2:3, :] = counts.astype(jnp.int32)
+    order[3:4, :] = jnp.broadcast_to(jnp.max(counts, axis=1, keepdims=True), (1, passages)).astype(jnp.int32)
+    heads = jnp.where((lane % GROUP == 0) & (lens > line * TB), 1.0, 0.0).astype(jnp.bfloat16)
+    order[4:5, :] = lax.dot_general(
+        jnp.ones((8, passages), jnp.bfloat16), heads, across_lanes, preferred_element_type=jnp.float32
+    )[0:1].astype(jnp.int32)
+    most = TILES * (256 * queries // (own.shape[0] * n))
+    number = lax.broadcasted_iota(jnp.int32, (8, queries), 1).astype(jnp.float32).astype(jnp.bfloat16)
+    index = lax.broadcasted_iota(jnp.int32, (queries, queries), 0).astype(jnp.float32)
+    over = jnp.broadcast_to(counts, (8, passages)) > most
+    over_flags = jnp.where(over, 1.0, 0.0)
+    over_spot = jnp.dot(over_flags.astype(jnp.bfloat16), before, preferred_element_type=jnp.float32)
+    over_hit = jnp.where(jnp.where(over, over_spot, -1.0)[0:1] == index, 1.0, 0.0).astype(jnp.bfloat16)
+    order[5:6, :] = lax.dot_general(number, over_hit, across_lanes, preferred_element_type=jnp.float32)[0:1].astype(
+        jnp.int32
+    )
+    over_count = jnp.sum(over_flags[0:1], axis=1, keepdims=True)
+    order[6:7, :] = jnp.broadcast_to(over_count, (1, passages)).astype(jnp.int32)
+    order[7:8, :] = jnp.zeros((1, passages), jnp.int32)
     to_order = pltpu.make_async_copy(order, order_s, order_sem)
     to_order.start()
     for b in range(4):
@@ -117,7 +151,7 @@
                 cent[at, :] = stage[at, :].astype(jnp.float32)
 
     widen(0, pieces // 2)
-    pl.semaphore_wait(barrier, line_size + wide - 2 + 3)
+    pl.semaphore_wait(barrier, line_size + wide)
 
     def remote(src, dst, send, recv, peer):
         return pltpu.make_async_remote_copy(
@@ -129,7 +163,8 @@
     for i in range(1, wide):
         remote(own, qall.at[mx, my, core], q_send, q_recv, in_column(i)).start()
     mid[mr] = wanted[mr]
-    qall[mx, my, core] = own[...]
+    keep_queries = pltpu.make_async_copy(own, qall.at[mx, my, core], own_sem.at[2])
+    keep_queries.start()
     widen(pieces // 2, pieces)
     to_order.wait()
     load_packed.wait()
@@ -141,6 +176,7 @@
         remote(mid.at[:, lax.rem(mx + i, wide)], asked.at[mx], row_send, row_recv, in_column(i)).start()
     asked[mx] = mid[:, mx]
     remote(qall.at[pl.ds(0, wide - 1), 0, 0], qall.at[pl.ds(0, wide - 1), 0, 0], q_send, q_recv, in_column(1)).wait_recv()
+    keep_queries.wait()
     for i in range(1, deep):
         peer = (mx * deep + lax.rem(my + i, deep)) * cores + core
         remote(qall.at[:, my, core], qall.at[:, my, core], q_row_send, q_row_recv, peer).start()
@@ -184,8 +220,6 @@
     def forward(owner):
         along(tab.at[owner, z], right, left_recv).start()
         along(tab.at[owner, z], left, right_recv).start()
-        if part < rows:
-            along(tab.at[owner, z, pl.ds(part, rows - part)], far, far_recv).start()
 
     def decode(i):
         words = packed[order_s[0, i]]
@@ -193,15 +227,22 @@
         low = jnp.where(digits == 0, spread[0], spread[1])
         high = jnp.where(digits == 2, spread[2], spread[3])
         value = jnp.where(digits < 2, low, high)
-        resid[lax.div(i, 8), pl.ds(lax.rem(i, 8), ptok, stride=8), :] = value.T
+        resid[i] = value.T
+
+    def enlist(i):
+        hit = jnp.where(spots[pl.ds(i, 1), :] == index, 1.0, 0.0).astype(jnp.bfloat16)
+        listed = lax.dot_general(number, hit, across_lanes, preferred_element_type=jnp.float32)
+        members[pl.ds(i, 1), :] = listed[0:1].astype(jnp.int32)
 
     def extras(k, peer):
         for j in range(passages // n):
             decode(k * (passages // n) + j)
+            enlist(k * (passages // n) + j)
         pull(k, peer, 1, rows, part)
 
     def save(g):
-        return pltpu.make_async_copy(resid.at[g], resid_hbm.at[g], resid_sem)
+        at = pl.ds(g * 8, 8)
+        return pltpu.make_async_copy(resid.at[at], resid_hbm.at[at], resid_sem)
 
     def bulk(ref, send, recv):
         return pltpu.make_async_remote_copy(
@@ -227,9 +268,6 @@
         def _():
             save(lax.div(k, 2)).start()
 
-    per = own.shape[0]
-    queries = qcols.shape[1] // tokens
-
     @pl.loop(1, n // 2)
     def _(k):
         relay(k)
@@ -238,31 +276,13 @@
     pair = remote(qall.at[:, :, core], qall.at[:, :, core], pair_send, pair_recv, me + 1 - 2 * core)
     pair.start()
 
-    @pl.loop(n // 2, n // 4 * 3)
+    @pl.loop(n // 2, n)
     def _(k):
         relay(k)
 
     pair.wait()
-
-    @pl.loop(0, wide)
-    def _(i):
-        for y in range(deep):
-            for c in range(cores):
-                at = i * (line_size * per) + (y * cores + c) * per
-                qwide[pl.ds(pl.multiple_of(at, per), per), :] = qall[i, y, c].astype(jnp.float32)
-
-    for t in range(tokens):
-        tile = qwide[pl.ds(t, queries, stride=tokens), :]
-        qcols[:, t * queries : (t + 1) * queries] = tile.T.astype(jnp.bfloat16)
-
-    @pl.loop(n // 4 * 3, n)
-    def _(k):
-        relay(k)
-
     bulk(tab.at[pl.ds(0, n // nz)], z_send, left_recv).wait_recv()
     bulk(tab.at[pl.ds(0, n // nz)], z_send, right_recv).wait_recv()
-    if part < rows:
-        bulk(tab.at[pl.ds(0, n), 0, pl.ds(part, rows - part)], z_send, far_recv).wait_recv()
     bulk(sbuf.at[pl.ds(0, n - 1), pl.ds(rows, part)], z_send, half_recv).wait_recv()
     keep_half.wait()
     pltpu.make_async_copy(resid, resid_hbm, resid_sem).wait()
@@ -272,11 +292,9 @@
     bulk(qall.at[pl.ds(0, wide), pl.ds(0, deep - 1), 0], q_row_send, q_row_recv).wait_send()
     bulk(sbuf.at[pl.ds(0, n - 1)], blk_send, q_recv).wait_send()
     bulk(tab.at[pl.ds(0, 2 * n // nz)], z_send, q_recv).wait_send()
-    if part < rows:
-        bulk(tab.at[pl.ds(0, n), 0, pl.ds(part, rows - part)], z_send, q_recv).wait_send()
-
-
-def fetch(centroids, wanted, own, lengths, packed, buckets, tokens):
+
+
+def fetch(centroids, wanted, own, lengths, packed, buckets, cand, live):
     n, nz = lax.axis_size("cent"), lax.axis_size("qry")
     wide, deep, cores = CENT_AXES
     rows = wanted.shape[3]
@@ -285,17 +303,19 @@
     vmem = pl.BlockSpec(memory_space=pltpu.VMEM)
     hbm = pl.BlockSpec(memory_space=pl.ANY)
     dma = pltpu.SemaphoreType.DMA
-    groups = passages // 8
+    queries = cand.shape[1]
     return pl.pallas_call(
-        functools.partial(fetch_kernel, tokens),
+        fetch_kernel,
         out_shape=(
             jax.ShapeDtypeStruct((n, nz, rows, 128), jnp.bfloat16),
-            jax.ShapeDtypeStruct((groups, 8 * ptok, 128), jnp.float32),
-            jax.ShapeDtypeStruct((128, n * own.shape[0]), jnp.bfloat16),
+            jax.ShapeDtypeStruct((passages, ptok, 128), jnp.float32),
+            jax.ShapeDtypeStruct(CENT_AXES + own.shape, jnp.bfloat16),
             jax.ShapeDtypeStruct((8, passages), jnp.int32),
+            jax.ShapeDtypeStruct((passages, queries), jnp.int32),
+            jax.ShapeDtypeStruct((passages, queries), jnp.int32),
         ),
-        in_specs=[hbm, vmem, vmem, vmem, hbm, vmem],
-        out_specs=(hbm, hbm, vmem, vmem),
+        in_specs=[hbm, vmem, vmem, vmem, hbm, vmem, vmem, vmem],
+        out_specs=(hbm, hbm, hbm, vmem, vmem, vmem),
         scratch_shapes=[
             pltpu.VMEM(packed.shape, jnp.int32),
             pltpu.VMEM(centroids.shape, jnp.bfloat16),
@@ -304,39 +324,31 @@
             pltpu.VMEM((wide, deep * cores, 2, rows), jnp.int32),
             pltpu.SMEM((wide, deep * cores, 2, rows), jnp.int32),
             pltpu.VMEM((n, rows + part, 128), jnp.bfloat16),
-            pltpu.VMEM(CENT_AXES + own.shape, jnp.bfloat16),
-            pltpu.VMEM((n * own.shape[0], 128), jnp.float32),
             pltpu.VMEM((4, 128, ptok), jnp.float32),
-            pltpu.VMEM((groups, 8 * ptok, 128), jnp.float32),
+            pltpu.VMEM((passages, ptok, 128), jnp.float32),
+            pltpu.VMEM((passages, queries), jnp.float32),
             pltpu.SMEM((8, passages), jnp.int32),
-            dma, dma((8,)), dma, dma, dma((2,)), dma, dma, dma, dma, dma,
-            dma, dma, dma, dma, dma, dma, dma, dma((n,)), dma, dma, dma, dma, dma,
+            dma, dma((8,)), dma, dma, dma((3,)), dma, dma, dma, dma, dma,
+            dma, dma, dma, dma, dma, dma, dma, dma((n,)), dma, dma, dma, dma,
         ],
         compiler_params=pltpu.CompilerParams(
             collective_id=0, has_side_effects=True, vmem_limit_bytes=58 * 2**20
         ),
-    )(centroids, wanted, own, lengths, packed, buckets)
+    )(centroids, wanted, own, lengths, packed, buckets, cand, live)
 
 
 def score_kernel(
-    refs, order, order_ref, table_hbm, resid_hbm, q_hbm, cand_ref, live_ref,
-    out_ref, stage, tab, resid, q_ref, first, acc, scores, len_ref, blk_g, blk_b, stage_sem, resid_sem, q_sem,
+    order, refs_hbm, members_hbm, order_ref, place_ref, table_hbm, resid_hbm, q_hbm, cand_ref, live_ref,
+    out_ref, refs, members, stage, tab, resid, q_ref, embeds, best, scores, refs_sem, members_sem, stage_sem, resid_sem, q_sem,
 ):
     passages = order.shape[1]
-    groups = passages // 8
-    columns = q_ref.shape[1]
+    groups = passages // GROUP
     slots, queries = cand_ref.shape
-    ptok = resid_hbm.shape[1] // 8
-    rows = TB * 8
+    ptok = resid_hbm.shape[1]
+    tokens = q_hbm.shape[0] // queries
+    wide = 256 // tokens
     pieces = stage_sem.shape[0]
     depth = stage.shape[0] // pieces
-
-    def load(i):
-        return pltpu.make_async_copy(
-            table_hbm.at[pl.ds(pl.multiple_of(i * depth, depth), depth)],
-            stage.at[lax.rem(i, 2)], stage_sem.at[lax.rem(i, 2)],
-        )
-
     loads = [
         pltpu.make_async_copy(
             table_hbm.at[i * depth : (i + 1) * depth], stage.at[i * depth : (i + 1) * depth], stage_sem.at[i]
@@ -345,35 +357,24 @@
     ]
     for load in loads:
         load.start()
-    load_q = pltpu.make_async_copy(q_hbm, q_ref, q_sem)
-    load_q.start()
+    load_refs = pltpu.make_async_copy(refs_hbm, refs, refs_sem)
+    load_refs.start()
 
     def load_resid(g):
-        return pltpu.make_async_copy(resid_hbm.at[g], resid.at[g], resid_sem.at[g])
+        at = pl.ds(g * GROUP, GROUP)
+        return pltpu.make_async_copy(resid_hbm.at[at], resid.at[at], resid_sem.at[g])
+
+    load_members = pltpu.make_async_copy(members_hbm, members, members_sem)
+    load_members.start()
 
     @pl.loop(0, groups)
     def _(g):
         load_resid(g).start()
 
-    acc[...] = jnp.full(acc.shape, LOW, jnp.float32)
-    spread = jnp.broadcast_to(order_ref[1:2, :], (passages, passages)).T
-    len_ref[...] = spread.reshape(groups, 8, 128)
-
-    def add_group(g, n):
-        count = lax.div(order[1, g * 8] + (TB - 1), TB)
-
-        def add(b, m):
-            blk_g[m] = g
-            blk_b[m] = b
-            return m + 1
-
-        return lax.fori_loop(0, count, add, n)
-
-    total = lax.fori_loop(0, groups, add_group, 0)
-    for extra in range(UNIT - 1):
-        blk_g[total + extra] = blk_g[total - 1]
-        blk_b[total + extra] = blk_b[total - 1]
-    steps = lax.div(total + (UNIT - 1), UNIT)
+    load_q = pltpu.make_async_copy(q_hbm, q_ref, q_sem)
+    load_q.start()
+
+    ends = [order[4, c] for c in range(ptok // TB)]
 
     for i, load in enumerate(loads):
         load.wait()
@@ -383,71 +384,93 @@
             at = pl.ds(pl.multiple_of(i * depth + j * 512, 512), 512)
             tab[at, :] = stage[at, :].astype(jnp.float32)
 
+    load_refs.wait()
+    load_resid(0).wait()
+    sub = lax.broadcasted_iota(jnp.int32, (8, 128), 0)
+
+    def embed(r, rows):
+        source = order[0, r] * ptok
+        tiles = []
+        for t in range(0, rows, 8):
+            tile = jnp.broadcast_to(tab[pl.ds(refs[source + t], 1), :], (8, 128))
+            for p in range(1, 8):
+                row = jnp.broadcast_to(tab[pl.ds(refs[source + t + p], 1), :], (8, 128))
+                tile = jnp.where(sub == p, row, tile)
+            tiles.append(tile)
+        summed = jnp.concatenate(tiles, axis=0) + resid[r, 0:rows, :]
+        norm = jnp.sum(summed * summed, axis=1, keepdims=True)
+        unit = summed * lax.rsqrt(norm + EPS)
+        line = lax.broadcasted_iota(jnp.int32, unit.shape, 0)
+        unit = jnp.where(line < order[1, r], unit, unit[0:1]).astype(jnp.bfloat16)
+        embeds[r, 0:rows, :] = unit
+        return unit
+
+    def weights(r, k):
+        parts = []
+        for j in range(wide):
+            at = pl.multiple_of(members[r, k * wide + j] * tokens, tokens)
+            parts.append(q_ref[pl.ds(at, tokens), :])
+        return jnp.concatenate(parts, axis=0)
+
+    def similar(unit, r, k):
+        return lax.dot_general(
+            unit, weights(r, k), (((1,), (1,)), ((), ())), preferred_element_type=jnp.float32
+        )
+
+    def step(g, units, rows):
+        @pl.when(g + 1 < groups)
+        def _():
+            load_resid(g + 1).wait()
+
+        following = []
+        for p in range(GROUP):
+            following.append(embed(jnp.minimum(g + 1, groups - 1) * GROUP + p, rows))
+            r = g * GROUP + p
+            for k in range(TILES):
+                sim = similar(units[p], r, k)
+                best[k, pl.ds(r, 1), :] = jnp.max(sim, axis=0, keepdims=True)
+        return tuple(following)
+
+    units = tuple(embed(p, ptok) for p in range(GROUP))
+    load_members.wait()
     load_q.wait()
-
-    def arrive(first_group, last_group):
-        @pl.loop(first_group, last_group + 1)
-        def _(g):
-            load_resid(g).wait()
-
-    arrive(0, blk_g[UNIT - 1])
-
-    def embed_one(u, i, head):
-        g, b = blk_g[i], blk_b[i]
-        where = [order[0, g * 8 + p] * ptok + b * TB for p in range(8)]
-        sub = lax.broadcasted_iota(jnp.int32, (8, 128), 0)
-        tiles = []
-        for t in range(TB):
-            tile = jnp.broadcast_to(tab[pl.ds(refs[where[0] + t], 1), :], (8, 128))
-            for p in range(1, 8):
-                tile = jnp.where(sub == p, jnp.broadcast_to(tab[pl.ds(refs[where[p] + t], 1), :], (8, 128)), tile)
-            tiles.append(tile)
-        got = jnp.concatenate(tiles, axis=0)
-        start = pl.multiple_of(b * rows, rows)
-        summed = got + resid[g, pl.ds(start, rows), :]
-        norm = jnp.sum(summed * summed, axis=1, keepdims=True)
-        unit = (summed * lax.rsqrt(norm + EPS)).reshape(TB, 8, 128)
-        head = jnp.where(b == 0, unit[0], head)
-        token = b * TB + lax.broadcasted_iota(jnp.int32, (TB, 8, 128), 0)
-        unit = jnp.where(token < len_ref[g][None], unit, head[None])
-        return unit.reshape(rows, 128).astype(jnp.bfloat16), head
-
-    def embed(s):
-        head = first[...]
-        units = []
-        for u in range(UNIT):
-            unit, head = embed_one(u, s * UNIT + u, head)
-            units.append(unit)
-        first[...] = head
-        return jnp.concatenate(units, axis=0)
-
-    def step(s, unit):
-        later = jnp.minimum(s + 1, steps - 1)
-        arrive(blk_g[s * UNIT + UNIT - 1] + 1, blk_g[later * UNIT + UNIT - 1])
-        group = [blk_g[s * UNIT + u] for u in range(UNIT)]
-        head = first[...]
-        following = []
-        parts = columns // CHUNK // UNIT
-        for part, c in enumerate(range(0, columns, CHUNK)):
-            if part % parts == 0:
-                u = part // parts
-                block, head = embed_one(u, later * UNIT + u, head)
-                following.append(block)
-            sim = jnp.dot(unit, q_ref[:, c : c + CHUNK], preferred_element_type=jnp.float32)
-            best = jnp.max(sim.reshape(UNIT, TB, 8, CHUNK), axis=1)
-            for u in range(UNIT):
-                acc[group[u], :, c : c + CHUNK] = jnp.maximum(acc[group[u], :, c : c + CHUNK], best[u])
-        first[...] = head
-        return jnp.concatenate(following, axis=0)
-
-    lax.fori_loop(0, steps, step, embed(0))
-
-    @pl.loop(0, groups)
-    def _(g):
-        total_sum = acc[g, :, 0:queries]
-        for t in range(1, columns // queries):
-            total_sum = total_sum + acc[g, :, t * queries : (t + 1) * queries]
-        scores[pl.ds(pl.multiple_of(g * 8, 8), 8), :] = total_sum
+    begin = 0
+    for c in range(ptok // TB, 0, -1):
+        units = tuple(unit[: c * TB] for unit in units)
+        units = lax.fori_loop(begin, ends[c - 1], lambda g, held, rows=c * TB: step(g, held, rows), units)
+        begin = ends[c - 1]
+
+    used = lax.div(order[3, 0] + wide - 1, wide)
+
+    @pl.loop(TILES, used)
+    def _(k):
+        best[k] = jnp.zeros(best.shape[1:], jnp.float32)
+
+    @pl.loop(0, order[6, 0])
+    def _(m):
+        r = order[5, m]
+
+        @pl.loop(TILES, lax.div(order[2, r] + wide - 1, wide))
+        def _(k):
+            sim = similar(embeds[r], r, k)
+            token = lax.broadcasted_iota(jnp.int32, sim.shape, 0)
+            sim = jnp.where(token < order[1, r], sim, LOW)
+            best[k, pl.ds(r, 1), :] = jnp.max(sim, axis=0, keepdims=True)
+
+    from_lane = lax.div(lax.broadcasted_iota(jnp.int32, (256, queries), 0), tokens)
+    to_lane = lax.broadcasted_iota(jnp.int32, (256, queries), 1)
+
+    def gather_sum(k, total_sum):
+        adder = (from_lane + k * wide == to_lane).astype(jnp.float32)
+        return total_sum + jnp.dot(
+            best[k], adder, precision=lax.Precision.HIGHEST, preferred_element_type=jnp.float32
+        )
+
+    sums = jnp.zeros((passages, queries), jnp.float32)
+    for k in range(TILES):
+        sums = gather_sum(k, sums)
+    sums = lax.fori_loop(TILES, used, gather_sum, sums)
+    scores[...] = jnp.take_along_axis(sums, place_ref[...], axis=1)
 
     cand = cand_ref[...]
 
@@ -468,36 +491,36 @@
     out_ref[...] = padded.T
 
 
-def score(table, refs, order, resid, qcols, cand, live):
-    groups = resid.shape[0]
+def score(table, refs, order, members, place, resid, rows, cand, live):
     passages = order.shape[1]
-    queries, slots = cand.shape
+    slots, queries = cand.shape
+    ptok = resid.shape[1]
     vmem = pl.BlockSpec(memory_space=pltpu.VMEM)
     smem = pl.BlockSpec(memory_space=pltpu.SMEM)
     hbm = pl.BlockSpec(memory_space=pl.ANY)
-    blocks = resid.shape[0] * resid.shape[1] // (8 * TB) + UNIT
     return pl.pallas_call(
         score_kernel,
         out_shape=jax.ShapeDtypeStruct((queries, 128), jnp.float32),
-        in_specs=[smem, smem, vmem, hbm, hbm, hbm, vmem, vmem],
+        in_specs=[smem, hbm, hbm, vmem, vmem, hbm, hbm, hbm, vmem, vmem],
         out_specs=vmem,
         scratch_shapes=[
+            pltpu.SMEM((passages * ptok,), jnp.int32),
+            pltpu.SMEM(members.shape, jnp.int32),
             pltpu.VMEM(table.shape, jnp.bfloat16),
             pltpu.VMEM((table.shape[0], 128), jnp.float32),
             pltpu.VMEM(resid.shape, jnp.float32),
-            pltpu.VMEM(qcols.shape, jnp.bfloat16),
-            pltpu.VMEM((8, 128), jnp.float32),
-            pltpu.VMEM((groups, 8, qcols.shape[1]), jnp.float32),
+            pltpu.VMEM(rows.shape, jnp.bfloat16),
+            pltpu.VMEM(resid.shape, jnp.bfloat16),
+            pltpu.VMEM((queries // 8, passages, 256), jnp.float32),
             pltpu.VMEM((passages, queries), jnp.float32),
-            pltpu.VMEM((groups, 8, 128), jnp.int32),
-            pltpu.SMEM((blocks,), jnp.int32),
-            pltpu.SMEM((blocks,), jnp.int32),
+            pltpu.SemaphoreType.DMA,
+            pltpu.SemaphoreType.DMA,
             pltpu.SemaphoreType.DMA((8,)),
-            pltpu.SemaphoreType.DMA((groups,)),
+            pltpu.SemaphoreType.DMA((passages // GROUP,)),
             pltpu.SemaphoreType.DMA,
         ],
         compiler_params=pltpu.CompilerParams(vmem_limit_bytes=56 * 2**20),
-    )(refs.reshape(-1), order, order, table, resid, qcols, cand.T, live[None, :])
+    )(order, refs.reshape(-1), members, order, place, table, resid, rows, cand, live)
 
 
 def swap_kernel(tops, inbox, outbox, mid, row_send, row_recv, send, recv):
@@ -628,11 +651,14 @@
         [lax.dynamic_slice_in_dim(by_owner, quarter, 1, 1) for quarter in (z, lax.rem(z + 2, nz))], axis=1
     )
     wanted = jnp.swapaxes(wanted.reshape((CENT_AXES[0], n // CENT_AXES[0]) + wanted.shape[1:]), 0, 1)
-    table, resid, qcols, order = fetch(
+    cand, live = candidates[0, 0].T, live_counts[0]
+    table, resid, rows, order, members, place = fetch(
         centroids, wanted, queries.reshape(per * tokens, width), passage_lengths[None, :], packed_residual_buckets,
-        bucket_values, tokens,
+        bucket_values, cand, live,
     )
-    tops = score(table.reshape(-1, width), token_refs, order, resid, qcols, candidates[0, 0], live_counts[0, 0])
+    tops = score(
+        table.reshape(-1, width), token_refs, order, members, place, resid, rows.reshape(-1, width), cand, live
+    )
     shard_tops, best_scores = merge(swap(tops, per), candidates.shape[3] // 4)
     return (jnp.transpose(shard_tops, (1, 2, 0))[None], best_scores[None])
 

time: 106 us -> 95.6 us (0.902)
  Pallas kernels: 103 us -> 92.9 us
    pallas_call x1, Pallas kernels: 14.8 us -> 10 us  [swap(): pl.pallas_call(swap_kernel, out_shape=jax.ShapeDtypeStruct((wide, deep *...]
    pallas_call x1, Pallas kernels: 34.4 us -> 30 us  [score(): pl.pallas_call(score_kernel, out_shape=jax.ShapeDtypeStruct((queries, 128...]
where the time goes in v4:
time: 95.6 us; the launch traced here: 95.2 us
  Pallas kernels  92.9 us (97%)
  local copies, waits for them, and re-layouts  1.57 us (2%)
    pallas_call x1, Pallas kernels, fetch(): pl.pallas_call(fetch_kernel, out_shape=(jax.ShapeDtypeStruct((n, nz, rows...  50.1 us
    pallas_call x1, Pallas kernels, score(): pl.pallas_call(score_kernel, out_shape=jax.ShapeDtypeStruct((queries, 128...  30 us
    pallas_call x1, Pallas kernels, swap(): pl.pallas_call(swap_kernel, out_shape=jax.ShapeDtypeStruct((wide, deep *...  10 us
    pallas_call x1, Pallas kernels, merge(): pl.pallas_call(merge_kernel, out_shape=(jax.ShapeDtypeStruct((keep, per,...  2.83 us

profile of v4, /device:TPU:1, one launch (start us, length us, event | category | flops | bytes accessed | tf_op | source)
XLA Modules:
  0.0 95.2 jit_solution(10499873019041579229)
XLA Ops:
  0.6 1.0 %constant_dynamic-slice_fusion.1 = (s32[32,1,128]{2,1,0:T(1,128)S(1)}, s32[32,1,128]{2,1,0:T(1,128)S(1)}) fusion(s32[32,4,128]{2,1,0:T(4,128)} %bitcast.28, s32[]{:T(128)S(6)} %select_n.6, s32[]{:T(128)S(6)} %select_n.7), kind=kLoop, calls=%fused_computation.3 | loop fusion | bytes 65544 | tf_op jit(solution)/shard_map/dynamic_slice | solution.py:651
  1.6 0.6 copy.17
  2.3 50.1 %shard_map.104 = (bf16[32,4,128,128]{3,2,1,0:T(8,128)(2,1)}, f32[128,128,128]{2,1,0:T(8,128)}, bf16[4,4,2,128,128]{4,3,2,1,0:T(8,128)(2,1)}, s32[8,128]{1,0:T(8,...) custom-call(bf16[32768,128]{1,0:T(8,128)(2,1)} %cent_hbm.1, s32[8,4,2,128]{3,2,1,0:T(2,128)} %bitcast.22, ...), custom_call_target="tpu_custom_call" | custom-call | tf_op jit(solution)/shard_map/pallas_call | solution.py:307
  52.4 30.0 %shard_map.105.tops = f32[128,128]{1,0:T(8,128)} custom-call(s32[8,128]{1,0:T(8,128)} %get-tuple-element.10.order.order_ref, s32[16384]{0:T(1024)} %bitcast.26, s32[128,128]{1,0:T(8,128)} %get-tuple-element.11.members_hbm, s32[8,128]{1,0:T(8,128)} %get-tuple-element.10.order.order_ref, s32[128,128]{1,0:T(8,128)} %get-tuple-element.12.place_ref, ...), custom_call_target="tpu_custom_call" | custom-call | tf_op jit(solution)/shard_map/pallas_call | solution.py:501
  82.3 10.0 %shard_map.106 = f32[4,8,4,128]{3,2,1,0:T(4,128)} custom-call(f32[128,128]{1,0:T(8,128)} %shard_map.105.tops), custom_call_target="tpu_custom_call" | custom-call | tf_op jit(solution)/shard_map/pallas_call | solution.py:572
  92.3 2.8 %shard_map.107 = (f32[12,4,32]{2,1,0:T(4,128)}, f32[4,100]{1,0:T(4,128)}) custom-call(f32[32,4,128]{2,1,0:T(4,128)} %bitcast.21), custom_call_target="tpu_custom_call" | custom-call | tf_op jit(solution)/shard_map/pallas_call | solution.py:624
  (1 shorter events, 0.0 us)

commit v5 on v4

--- a/solution.py
+++ b/solution.py
@@ -159,17 +159,17 @@
         )
 
     for i in range(1, line_size):
-        remote(wanted.at[lax.rem(mr + i, line_size)], mid.at[mr], off_send, off_recv, in_row(i)).start()
+        remote(wanted.at[:, lax.rem(mr + i, line_size)], mid.at[mr], off_send, off_recv, in_row(i)).start()
     for i in range(1, wide):
         remote(own, qall.at[mx, my, core], q_send, q_recv, in_column(i)).start()
-    mid[mr] = wanted[mr]
+    mid[mr] = wanted[:, mr]
     keep_queries = pltpu.make_async_copy(own, qall.at[mx, my, core], own_sem.at[2])
     keep_queries.start()
     widen(pieces // 2, pieces)
     to_order.wait()
     load_packed.wait()
     first = remote(
-        wanted.at[pl.ds(0, line_size - 1)], mid.at[pl.ds(0, line_size - 1)], off_send, off_recv, in_row(1)
+        mid.at[pl.ds(0, line_size - 1)], mid.at[pl.ds(0, line_size - 1)], off_send, off_recv, in_row(1)
     )
     first.wait_recv()
     for i in range(1, wide):
@@ -184,9 +184,14 @@
         asked.at[pl.ds(0, wide - 1)], asked.at[pl.ds(0, wide - 1)], row_send, row_recv, in_column(1)
     )
     second.wait_recv()
-    to_scalar = pltpu.make_async_copy(asked, asked_s, asked_sem)
-    to_scalar.start()
-    to_scalar.wait()
+    to_scalar = [
+        pltpu.make_async_copy(asked.at[:, :, quarter], asked_s.at[:, :, line_at], asked_sem.at[line_at])
+        for line_at, quarter in enumerate((z, far))
+    ]
+    for copy in to_scalar:
+        copy.start()
+    for copy in to_scalar:
+        copy.wait()
 
     sub = lax.broadcasted_iota(jnp.int32, (16, 128), 0)
 
@@ -320,15 +325,15 @@
             pltpu.VMEM(packed.shape, jnp.int32),
             pltpu.VMEM(centroids.shape, jnp.bfloat16),
             pltpu.VMEM(centroids.shape, jnp.float32),
-            pltpu.VMEM((deep * cores, wide, 2, rows), jnp.int32),
-            pltpu.VMEM((wide, deep * cores, 2, rows), jnp.int32),
+            pltpu.VMEM((deep * cores, wide, nz, rows), jnp.int32),
+            pltpu.VMEM((wide, deep * cores, nz, rows), jnp.int32),
             pltpu.SMEM((wide, deep * cores, 2, rows), jnp.int32),
             pltpu.VMEM((n, rows + part, 128), jnp.bfloat16),
             pltpu.VMEM((4, 128, ptok), jnp.float32),
             pltpu.VMEM((passages, ptok, 128), jnp.float32),
             pltpu.VMEM((passages, queries), jnp.float32),
             pltpu.SMEM((8, passages), jnp.int32),
-            dma, dma((8,)), dma, dma, dma((3,)), dma, dma, dma, dma, dma,
+            dma, dma((8,)), dma((2,)), dma, dma((3,)), dma, dma, dma, dma, dma,
             dma, dma, dma, dma, dma, dma, dma, dma((n,)), dma, dma, dma, dma,
         ],
         compiler_params=pltpu.CompilerParams(
@@ -355,29 +360,30 @@
         )
         for i in range(pieces)
     ]
+    load_refs = pltpu.make_async_copy(refs_hbm, refs, refs_sem)
+    load_refs.start()
     for load in loads:
         load.start()
-    load_refs = pltpu.make_async_copy(refs_hbm, refs, refs_sem)
-    load_refs.start()
 
     def load_resid(g):
         at = pl.ds(g * GROUP, GROUP)
         return pltpu.make_async_copy(resid_hbm.at[at], resid.at[at], resid_sem.at[g])
 
     load_members = pltpu.make_async_copy(members_hbm, members, members_sem)
-    load_members.start()
-
-    @pl.loop(0, groups)
-    def _(g):
-        load_resid(g).start()
-
     load_q = pltpu.make_async_copy(q_hbm, q_ref, q_sem)
-    load_q.start()
+    load_resid(0).start()
 
     ends = [order[4, c] for c in range(ptok // TB)]
 
     for i, load in enumerate(loads):
         load.wait()
+        if i == pieces - 2:
+            load_members.start()
+            load_q.start()
+
+            @pl.loop(1, groups)
+            def _(g):
+                load_resid(g).start()
 
         @pl.loop(0, depth // 512)
         def _(j):
@@ -523,7 +529,7 @@
     )(order, refs.reshape(-1), members, order, place, table, resid, rows, cand, live)
 
 
-def swap_kernel(tops, inbox, outbox, mid, row_send, row_recv, send, recv):
+def swap_kernel(tops_hbm, inbox, tops, outbox, mid, tops_sem, row_send, row_recv, send, recv):
     me, z = lax.axis_index("cent"), lax.axis_index("qry")
     wide, deep, cores = CENT_AXES
     line_size = deep * cores
@@ -536,11 +542,14 @@
     def in_column(i):
         return lax.rem(mx + i, wide) * line_size + mr
 
+    load = pltpu.make_async_copy(tops_hbm, tops, tops_sem)
+    load.start()
     barrier = pltpu.get_barrier_semaphore()
     for i in range(1, line_size):
         pl.semaphore_signal(barrier, inc=1, device_id=(in_row(i), z), device_id_type=MESH)
     for i in range(1, wide):
         pl.semaphore_signal(barrier, inc=1, device_id=(in_column(i), z), device_id_type=MESH)
+    load.wait()
     for x in range(wide):
         for r in range(line_size):
             at = (x * line_size + r) * per
@@ -568,16 +577,18 @@
     n = lax.axis_size("cent")
     wide, deep, cores = CENT_AXES
     vmem = pl.BlockSpec(memory_space=pltpu.VMEM)
+    hbm = pl.BlockSpec(memory_space=pl.ANY)
     dma = pltpu.SemaphoreType.DMA
     inbox = pl.pallas_call(
         swap_kernel,
         out_shape=jax.ShapeDtypeStruct((wide, deep * cores, per, 128), jnp.float32),
-        in_specs=[vmem],
+        in_specs=[hbm],
         out_specs=vmem,
         scratch_shapes=[
+            pltpu.VMEM(tops.shape, jnp.float32),
             pltpu.VMEM((deep * cores, wide, per, 128), jnp.float32),
             pltpu.VMEM((deep * cores, wide, per, 128), jnp.float32),
-            dma, dma, dma, dma,
+            dma, dma, dma, dma, dma,
         ],
         compiler_params=pltpu.CompilerParams(collective_id=1, has_side_effects=True),
     )(tops)
@@ -645,12 +656,7 @@
 ):
     n, nz = lax.axis_size("cent"), lax.axis_size("qry")
     per, tokens, width = queries.shape[1:]
-    z = lax.axis_index("qry")
-    by_owner = shard_table.reshape(n, nz, -1)
-    wanted = jnp.concatenate(
-        [lax.dynamic_slice_in_dim(by_owner, quarter, 1, 1) for quarter in (z, lax.rem(z + 2, nz))], axis=1
-    )
-    wanted = jnp.swapaxes(wanted.reshape((CENT_AXES[0], n // CENT_AXES[0]) + wanted.shape[1:]), 0, 1)
+    wanted = shard_table.reshape(CENT_AXES[0], n // CENT_AXES[0], nz, -1)
     cand, live = candidates[0, 0].T, live_counts[0]
     table, resid, rows, order, members, place = fetch(
         centroids, wanted, queries.reshape(per * tokens, width), passage_lengths[None, :], packed_residual_buckets,

time: 95.6 us -> 92.4 us (0.967)
  local copies, waits for them, and re-layouts: 1.57 us -> 0 us
  Pallas kernels: 92.9 us -> 91.4 us
where the time goes in v5:
time: 92.4 us; the launch traced here: 92.1 us
  Pallas kernels  91.4 us (99%)
    pallas_call x1, Pallas kernels, fetch(): pl.pallas_call(fetch_kernel, out_shape=(jax.ShapeDtypeStruct((n, nz, rows...  50.3 us
    pallas_call x1, Pallas kernels, score(): pl.pallas_call(score_kernel, out_shape=jax.ShapeDtypeStruct((queries, 128...  29.2 us
    pallas_call x1, Pallas kernels, swap(): pl.pallas_call(swap_kernel, out_shape=jax.ShapeDtypeStruct((wide, deep *...  9.11 us
    pallas_call x1, Pallas kernels, merge(): pl.pallas_call(merge_kernel, out_shape=(jax.ShapeDtypeStruct((keep, per,...  2.83 us

profile of v5, /device:TPU:1, one launch (start us, length us, event | category | flops | bytes accessed | tf_op | source)
XLA Modules:
  0.0 92.1 jit_solution(7822464015855516082)
XLA Ops:
  0.6 50.3 %shard_map.104 = (bf16[32,4,128,128]{3,2,1,0:T(8,128)(2,1)}, f32[128,128,128]{2,1,0:T(8,128)}, bf16[4,4,2,128,128]{4,3,2,1,0:T(8,128)(2,1)}, s32[8,128]{1,0:T(8,...) custom-call(bf16[32768,128]{1,0:T(8,128)(2,1)} %cent_hbm.1, s32[4,8,4,128]{3,2,1,0:T(4,128)} %bitcast.20, ...), custom_call_target="tpu_custom_call" | custom-call | tf_op jit(solution)/shard_map/pallas_call | solution.py:312
  50.9 29.2 %shard_map.105.tops_hbm = f32[128,128]{1,0:T(8,128)} custom-call(s32[8,128]{1,0:T(8,128)} %get-tuple-element.10.order.order_ref, s32[16384]{0:T(1024)} %bitcast.21, s32[128,128]{1,0:T(8,128)} %get-tuple-element.11.members_hbm, s32[8,128]{1,0:T(8,128)} %get-tuple-element.10.order.order_ref, s32[128,128]{1,0:T(8,128)} %get-tuple-element.12.place_ref, ...), custom_call_target="tpu_custom_call" | custom-call | tf_op jit(solution)/shard_map/pallas_call | solution.py:507
  80.1 9.1 %shard_map.106 = f32[4,8,4,128]{3,2,1,0:T(4,128)} custom-call(f32[128,128]{1,0:T(8,128)} %shard_map.105.tops_hbm), custom_call_target="tpu_custom_call" | custom-call | tf_op jit(solution)/shard_map/pallas_call | solution.py:582
  89.2 2.8 %shard_map.107 = (f32[12,4,32]{2,1,0:T(4,128)}, f32[4,100]{1,0:T(4,128)}) custom-call(f32[32,4,128]{2,1,0:T(4,128)} %bitcast.17), custom_call_target="tpu_custom_call" | custom-call | tf_op jit(solution)/shard_map/pallas_call | solution.py:635

commit v6 on v5

--- a/solution.py
+++ b/solution.py
@@ -160,8 +160,15 @@
 
     for i in range(1, line_size):
         remote(wanted.at[:, lax.rem(mr + i, line_size)], mid.at[mr], off_send, off_recv, in_row(i)).start()
+    half = own.shape[0] // 2
+    upper, lower = pl.ds(0, half), pl.ds(half, half)
+
+    def beside(i):
+        return (mx * deep + lax.rem(my + i, deep)) * cores + core
+
     for i in range(1, wide):
-        remote(own, qall.at[mx, my, core], q_send, q_recv, in_column(i)).start()
+        remote(own.at[upper], qall.at[mx, my, core, upper], q_send, q_recv, in_column(i)).start()
+        remote(own.at[lower], qall.at[mx, my, core, lower], q_send, q_recv, beside(i)).start()
     mid[mr] = wanted[:, mr]
     keep_queries = pltpu.make_async_copy(own, qall.at[mx, my, core], own_sem.at[2])
     keep_queries.start()
@@ -178,8 +185,9 @@
     remote(qall.at[pl.ds(0, wide - 1), 0, 0], qall.at[pl.ds(0, wide - 1), 0, 0], q_send, q_recv, in_column(1)).wait_recv()
     keep_queries.wait()
     for i in range(1, deep):
-        peer = (mx * deep + lax.rem(my + i, deep)) * cores + core
-        remote(qall.at[:, my, core], qall.at[:, my, core], q_row_send, q_row_recv, peer).start()
+        corner, side_row = qall.at[:, my, core, upper], qall.at[mx, :, core, lower]
+        remote(corner, corner, q_row_send, q_row_recv, beside(i)).start()
+        remote(side_row, side_row, q_row_send, q_row_recv, in_column(i)).start()
     second = remote(
         asked.at[pl.ds(0, wide - 1)], asked.at[pl.ds(0, wide - 1)], row_send, row_recv, in_column(1)
     )

time: 92.4 us -> 89 us (0.963)
  Pallas kernels: 91.4 us -> 88.1 us
    pallas_call x1, Pallas kernels: 50.3 us -> 46.6 us  [fetch(): pl.pallas_call(fetch_kernel, out_shape=(jax.ShapeDtypeStruct((n, nz, rows...]
    pallas_call x1, Pallas kernels: 9.11 us -> 11.4 us  [swap(): pl.pallas_call(swap_kernel, out_shape=jax.ShapeDtypeStruct((wide, deep *...]
    pallas_call x1, Pallas kernels: 29.2 us -> 27.3 us  [score(): pl.pallas_call(score_kernel, out_shape=jax.ShapeDtypeStruct((queries, 128...]
where the time goes in v6:
time: 89 us; the launch traced here: 88.8 us
  Pallas kernels  88.1 us (99%)
    pallas_call x1, Pallas kernels, fetch(): pl.pallas_call(fetch_kernel, out_shape=(jax.ShapeDtypeStruct((n, nz, rows...  46.6 us
    pallas_call x1, Pallas kernels, score(): pl.pallas_call(score_kernel, out_shape=jax.ShapeDtypeStruct((queries, 128...  27.3 us
    pallas_call x1, Pallas kernels, swap(): pl.pallas_call(swap_kernel, out_shape=jax.ShapeDtypeStruct((wide, deep *...  11.4 us
    pallas_call x1, Pallas kernels, merge(): pl.pallas_call(merge_kernel, out_shape=(jax.ShapeDtypeStruct((keep, per,...  2.83 us

profile of v6, /device:TPU:1, one launch (start us, length us, event | category | flops | bytes accessed | tf_op | source)
XLA Modules:
  0.0 88.8 jit_solution(2810465631230306437)
XLA Ops:
  0.6 46.6 %shard_map.104 = (bf16[32,4,128,128]{3,2,1,0:T(8,128)(2,1)}, f32[128,128,128]{2,1,0:T(8,128)}, bf16[4,4,2,128,128]{4,3,2,1,0:T(8,128)(2,1)}, s32[8,128]{1,0:T(8,...) custom-call(bf16[32768,128]{1,0:T(8,128)(2,1)} %cent_hbm.1, s32[4,8,4,128]{3,2,1,0:T(4,128)} %bitcast.20, ...), custom_call_target="tpu_custom_call" | custom-call | tf_op jit(solution)/shard_map/pallas_call | solution.py:320
  47.2 27.3 %shard_map.105.tops_hbm = f32[128,128]{1,0:T(8,128)} custom-call(s32[8,128]{1,0:T(8,128)} %get-tuple-element.10.order.order_ref, s32[16384]{0:T(1024)} %bitcast.21, s32[128,128]{1,0:T(8,128)} %get-tuple-element.11.members_hbm, s32[8,128]{1,0:T(8,128)} %get-tuple-element.10.order.order_ref, s32[128,128]{1,0:T(8,128)} %get-tuple-element.12.place_ref, ...), custom_call_target="tpu_custom_call" | custom-call | tf_op jit(solution)/shard_map/pallas_call | solution.py:515
  74.5 11.4 %shard_map.106 = f32[4,8,4,128]{3,2,1,0:T(4,128)} custom-call(f32[128,128]{1,0:T(8,128)} %shard_map.105.tops_hbm), custom_call_target="tpu_custom_call" | custom-call | tf_op jit(solution)/shard_map/pallas_call | solution.py:590
  85.9 2.8 %shard_map.107 = (f32[12,4,32]{2,1,0:T(4,128)}, f32[4,100]{1,0:T(4,128)}) custom-call(f32[32,4,128]{2,1,0:T(4,128)} %bitcast.17), custom_call_target="tpu_custom_call" | custom-call | tf_op jit(solution)/shard_map/pallas_call | solution.py:643
